TPU v7x, 32 devices: a whole 2x2x4 slice. The times are simulated.
32 devices in a mesh: cfg: 2 (over core), blk: 4 (over z), req: 4 (over y, x).
Axes of the slice: x: 2, y: 2, z: 4, core: 2. Of those that a mesh axis runs over, the one named last changes fastest.
Arguments:
- residual: bfloat16 [2, 16, 2048], P('cfg'), may hold values from -6 to 6
- queries: bfloat16 [2, 16, 4096], P('cfg', 'req'), may hold values from -80 to 80
- new_entries: bfloat16 [2, 16, 2, 2048], P('cfg', 'req'), may hold values from -6 to 6
- key_cache: bfloat16 [2, 16, 192, 2048], P('cfg', 'req', 'blk'), may hold values from -6 to 6
- value_cache: bfloat16 [2, 16, 192, 2048], P('cfg', 'req', 'blk'), may hold values from -8 to 8
- lengths: int32 [2, 16], P('cfg', 'req'), may hold values from 2 to 192, as said below
- attention_ids: int32 [16, 2], replicated, may hold values from 0 to 7, all different within a row
- expert_ids: int32 [16, 2], replicated, may hold values from 0 to 7, all different within a row
- attention_router: bfloat16 [2048, 8], replicated, may hold values from -0.125 to 0.125
- expert_router: bfloat16 [2048, 8], replicated, may hold values from -0.125 to 0.125
- attention_output: bfloat16 [16384, 2048], P(('blk', 'req')), may hold values from -0.125 to 0.125
- expert_gain: bfloat16 [2048], replicated, may hold values from 0.25 to 1.75
- expert_gate: bfloat16 [45056, 2048], P(('blk', 'req')), may hold values from -0.125 to 0.125
- expert_up: bfloat16 [45056, 2048], P(('blk', 'req')), may hold values from -0.125 to 0.125
- expert_down: bfloat16 [45056, 2048], P(('blk', 'req')), may hold values from -0.078125 to 0.078125
- final_gain: bfloat16 [2048], replicated, may hold values from 0.25 to 1.75
- unembedding: bfloat16 [32000, 2048], P(('blk', 'req')), may hold values from -0.125 to 0.125
- tenant_sizes: int32 [4], replicated, may hold values from 1 to 8, 16 in all
- guidance: int32 [4], replicated, may hold values from 2 to 16
Outputs:
- guided: float32 [16, 32000], P('cfg', ('blk', 'req'))
Inputs may be any that keep to these rules, and one draw needn't show every extreme that they name: lengths[0, i] lies from 96 to 192 and lengths[0, 0] = 192; lengths[1, i] lies from 2 to 48 and lengths[1, 0] = 48. `tenant_sizes`: the sizes sum to 16; the largest is exactly 8. `attention_ids`: the ids of one request differ. `expert_ids`: the ids of one request differ.
All inputs are finite; a program needn't handle non-finite values.
Results may differ from a plain program's by a relative error of at most 0.017.
Values may be sent and summed in bfloat16 or wider, within the bound.
A program may use at most 128 MiB of HBM per device.

v0:
```python
import math

import jax
import jax.numpy as jnp
from jax import lax
from jax.sharding import PartitionSpec as P

H = 16
HD = 128
FF = 5632
TOPK = 2


EPS = 1e-05


def joined(shard, axis, combine):
    everything = jax.tree.map(
        lambda part, kind: lax.all_gather(part.astype(kind), axis),
        shard,
        (jnp.bfloat16, jnp.bfloat16, jnp.bfloat16),
    )

    def take(k):
        return jax.tree.map(lambda part, own: part[k].astype(own.dtype), everything, shard)

    return lax.fori_loop(
        1, lax.axis_size(axis), lambda k, so_far: combine(so_far, take(k)), take(0)
    )


def swapped(value, axis, bit):
    mask = 2**bit
    pairs = [(source, source ^ mask) for source in range(lax.axis_size(axis))]
    return lax.ppermute(value, axis, pairs)


def rms_scale(values):
    return values * lax.rsqrt(jnp.mean(values * values, axis=-1, keepdims=True) + EPS)


def pair_gates(logits, chosen_ids):
    experts = jnp.arange(logits.shape[-1])
    picked = jnp.sum(
        jnp.where(chosen_ids[:, :, None] == experts[None, None, :], logits[:, None, :], 0.0),
        axis=-1,
    )
    first = jax.nn.sigmoid(picked[:, 0] - picked[:, 1])
    second = jax.nn.sigmoid(picked[:, 1] - picked[:, 0])
    return jnp.stack([first, second], axis=1)


def merge_parts(first_part, second_part):
    top_first, sum_first, acc_first = first_part
    top_second, sum_second, acc_second = second_part
    highest = jnp.maximum(top_first, top_second)
    scale_first = jnp.exp(top_first - highest)
    scale_second = jnp.exp(top_second - highest)
    merged_sum = sum_first * scale_first + sum_second * scale_second
    merged_acc = acc_first * scale_first[..., None] + acc_second * scale_second[..., None]
    return (highest, merged_sum, merged_acc)


def local(
    residual,
    queries,
    new_entries,
    key_cache,
    value_cache,
    lengths,
    attention_ids,
    expert_ids,
    attention_router,
    expert_router,
    attention_output,
    expert_gain,
    expert_gate,
    expert_up,
    expert_down,
    final_gain,
    unembedding,
    tenant_sizes,
    guidance,
):
    factor_scale = 1.0 / math.sqrt(HD)
    slot_rows = queries.shape[1]
    positions_local = key_cache.shape[2]
    feature_width = H * HD
    blk_index = lax.axis_index("blk")
    linear_index = blk_index * lax.axis_size("req") + lax.axis_index("req")
    query_heads = queries[0].reshape(slot_rows, TOPK, H, HD)
    key_heads = key_cache[0].reshape(slot_rows, positions_local, H, HD)
    value_heads = value_cache[0].reshape(slot_rows, positions_local, H, HD)
    scores = (
        jnp.einsum("rkhd,rphd->rkhp", query_heads, key_heads, preferred_element_type=jnp.float32)
        * factor_scale
    )
    positions = blk_index * positions_local + jnp.arange(positions_local)
    live = (positions[None, :] < lengths[0][:, None])[:, None, None, :]
    local_top = jnp.max(jnp.where(live, scores, -1e30), axis=-1)
    weights_local = jnp.where(live, jnp.exp(scores - local_top[..., None]), 0.0)
    weight_sums = jnp.sum(weights_local, axis=-1)
    weighted = jnp.einsum(
        "rkhp,rphd->rkhd",
        weights_local.astype(jnp.bfloat16),
        value_heads,
        preferred_element_type=jnp.float32,
    )
    highest, weight_sums, weighted = joined((local_top, weight_sums, weighted), "blk", merge_parts)
    new_keys = new_entries[0][:, 0].reshape(slot_rows, H, HD)
    new_values = new_entries[0][:, 1].reshape(slot_rows, H, HD)
    new_score = (
        jnp.einsum("rkhd,rhd->rkh", query_heads, new_keys, preferred_element_type=jnp.float32)
        * factor_scale
    )
    peak = jnp.maximum(highest, new_score)
    shrink = jnp.exp(highest - peak)
    fresh = jnp.exp(new_score - peak)
    denominator = weight_sums * shrink + fresh
    fresh_rounded = fresh.astype(jnp.bfloat16)
    numerator = weighted * shrink[..., None] + jnp.einsum(
        "rkh,rhd->rkhd", fresh_rounded, new_values, preferred_element_type=jnp.float32
    )
    attention_out = (
        (numerator / denominator[..., None])
        .astype(jnp.bfloat16)
        .reshape(slot_rows, TOPK, feature_width)
    )
    inputs = residual[0].astype(jnp.float32)
    normed_input = rms_scale(inputs).astype(jnp.bfloat16)
    attention_gates = pair_gates(
        jnp.dot(normed_input, attention_router, preferred_element_type=jnp.float32), attention_ids
    )
    proj_rows = attention_output.shape[0]
    first_row = linear_index * proj_rows
    own_expert = first_row // feature_width
    own_column = first_row % feature_width
    picked = (attention_ids == own_expert).astype(jnp.float32) * attention_gates
    columns = lax.dynamic_slice_in_dim(
        lax.all_gather(attention_out, "req", axis=0, tiled=True), own_column, proj_rows, 2
    ).astype(jnp.float32)
    selected = jnp.sum(picked[:, :, None] * columns, axis=1).astype(jnp.bfloat16)
    proj_terms = jnp.dot(selected, attention_output, preferred_element_type=jnp.float32)
    attention_proj = lax.psum(proj_terms, ("blk", "req"))
    middle = inputs + attention_proj
    expert_input = (rms_scale(middle) * expert_gain.astype(jnp.float32)).astype(jnp.bfloat16)
    expert_gates = pair_gates(
        jnp.dot(expert_input, expert_router, preferred_element_type=jnp.float32), expert_ids
    )
    hidden_rows = expert_gate.shape[0]
    hidden_expert = linear_index * hidden_rows // FF
    expert_share = jnp.sum((expert_ids == hidden_expert).astype(jnp.float32) * expert_gates, axis=1)
    gate_values = jnp.einsum(
        "rd,fd->rf", expert_input, expert_gate, preferred_element_type=jnp.float32
    )
    up_values = jnp.einsum("rd,fd->rf", expert_input, expert_up, preferred_element_type=jnp.float32)
    expert_hidden = (jax.nn.silu(gate_values) * up_values * expert_share[:, None]).astype(
        jnp.bfloat16
    )
    expert_terms = jnp.dot(expert_hidden, expert_down, preferred_element_type=jnp.float32)
    expert_out = lax.psum(expert_terms, ("blk", "req"))
    final_input = (rms_scale(middle + expert_out) * final_gain.astype(jnp.float32)).astype(
        jnp.bfloat16
    )
    logits = jnp.einsum("rd,vd->rv", final_input, unembedding, preferred_element_type=jnp.float32)
    stream_index = lax.axis_index("cfg")
    half_rows = logits.shape[0] // 2
    own_rows = lax.dynamic_slice_in_dim(logits, stream_index * half_rows, half_rows, 0)
    other_rows = lax.dynamic_slice_in_dim(logits, (1 - stream_index) * half_rows, half_rows, 0)
    partner = swapped(other_rows, "cfg", 0)
    first_stream = stream_index == 0
    conditional = jnp.where(first_stream, own_rows, partner)
    unconditional = jnp.where(first_stream, partner, own_rows)
    request_index = stream_index * half_rows + jnp.arange(half_rows)
    tenant_ends = jnp.cumsum(tenant_sizes)
    tenant = jnp.sum((request_index[:, None] >= tenant_ends[None, :]).astype(jnp.int32), axis=1)
    tenant_onehot = tenant[:, None] == jnp.arange(tenant_sizes.shape[0])[None, :]
    factor = (
        jnp.sum(jnp.where(tenant_onehot, guidance[None, :], 0), axis=1).astype(jnp.float32) / 4.0
    )
    return unconditional + factor[:, None] * (conditional - unconditional)


def solution(mesh):
    placed = (
        P("cfg", None, None),
        P("cfg", "req", None),
        P("cfg", "req", None, None),
        P("cfg", "req", "blk", None),
        P("cfg", "req", "blk", None),
        P("cfg", "req"),
        P(),
        P(),
        P(),
        P(),
        P(("blk", "req"), None),
        P(),
        P(("blk", "req"), None),
        P(("blk", "req"), None),
        P(("blk", "req"), None),
        P(),
        P(("blk", "req"), None),
        P(),
        P(),
    )
    return jax.shard_map(
        local, mesh=mesh, in_specs=placed, out_specs=P("cfg", ("blk", "req")), check_vma=False
    )
```

profile of v0, /device:TPU:0, one launch (start us, length us, event | category | flops | bytes accessed | tf_op | source)
XLA Modules:
  0.0 313.6 jit_solution(9471439564745491968)
XLA Ops:
  6.6 0.8 copy.72
  7.4 1.3 copy.71
  8.7 1.3 copy.73
  10.0 0.8 slice_convert_fusion
  10.8 1.0 fusion.32
  11.8 0.7 broadcast_compare_fusion
  12.5 0.6 select_reduce_fusion
  13.1 0.3 fusion.38
  13.4 0.4 fusion.6
  13.8 15.1 %all-gather.2 = bf16[16,2,16,128]{3,2,1,0:T(8,128)(2,1)S(1)} all-gather(bf16[4,2,16,128]{3,2,1,0:T(8,128)(2,1)S(1)} %copy.68), channel_id=4, replica_groups=mesh['cfg'=2,'blk'=4,'req'=4] {'blk'}, dimensions={0}, use_global_device_ids=true | all-gather | bytes 163840 | tf_op jit(solution)/shard_map/all_gather | solution.py:19
  29.0 11.9 %all-gather.1 = bf16[16,2,16]{2,1,0:T(2,128)(2,1)S(1)} all-gather(bf16[4,2,16]{2,1,0:T(2,128)(2,1)S(1)} %copy.66), channel_id=3, replica_groups=mesh['cfg'=2,'blk'=4,'req'=4] {'blk'}, dimensions={0}, use_global_device_ids=true | all-gather | bytes 1280 | tf_op jit(solution)/shard_map/all_gather | solution.py:19
  41.0 11.9 %all-gather = bf16[16,2,16]{2,1,0:T(2,128)(2,1)S(1)} all-gather(bf16[4,2,16]{2,1,0:T(2,128)(2,1)S(1)} %copy.64), channel_id=2, replica_groups=mesh['cfg'=2,'blk'=4,'req'=4] {'blk'}, dimensions={0}, use_global_device_ids=true | all-gather | bytes 1280 | tf_op jit(solution)/shard_map/all_gather | solution.py:19
  52.8 0.5 while.19
  53.6 8.5 %all_gather.21 = bf16[16,2,2048]{2,1,0:T(2,128)(2,1)S(1)} all-gather(bf16[4,2,2048]{2,1,0:T(2,128)(2,1)S(1)} %reshape.139), channel_id=1, replica_groups=mesh['cfg'=2,'blk'=4,'req'=4] {'req'}, dimensions={0}, use_global_device_ids=true | all-gather | bytes 163840 | tf_op jit(solution)/shard_map/all_gather | solution.py:140
  62.1 1.0 fusion.15
  63.0 1.0 fusion.20
  64.1 0.7 select_reduce_fusion.2
  64.8 0.7 compare_select_fusion.1
  65.6 0.2 multiply_reduce_fusion.2
  65.8 3.5 %fusion.46 = f32[16,2048]{1,0:T(8,128)} fusion(bf16[16,1024]{1,0:T(8,128)(2,1)S(1)} %multiply_reduce_fusion.2, bf16[1024,2048]{1,0:T(8,128)(2,1)} %param.31), kind=kOutput, calls=%fused_computation.93 | convolution fusion | flops 67108864 | bytes 4358144 | tf_op jit(solution)/shard_map/dot_general | solution.py:143
  69.5 0.2 reduce-window.8
  69.7 102.0 %all-reduce.3.cloned.1.call-done = f32[16,2048]{1,0:T(8,128)} async-done(((f32[16,2048]{1,0:T(8,128)}), f32[16,2048]{1,0:T(8,128)}) %all-reduce.3.cloned.1.call-update) | async-done | bytes 131088 | tf_op jit(solution)/shard_map/psum | solution.py:144
  171.6 1.0 multiply_reduce_fusion.1
  172.7 1.0 multiply_convert_fusion.1
  173.7 0.1 fusion.45
  173.9 7.4 %fusion.44 = f32[16,2816]{1,0:T(8,128)S(1)} fusion(bf16[16,2048]{1,0:T(8,128)(2,1)S(1)} %multiply_convert_fusion.1, bf16[2816,2048]{1,0:T(8,128)(2,1)} %param.33), kind=kOutput, calls=%fused_computation.91 | convolution fusion | flops 184549376 | bytes 11780096 | tf_op jit(solution)/shard_map/rd,fd->rf/dot_general | solution.py:153
  181.3 13.3 %fusion.9 = f32[16,2048]{1,0:T(8,128)} fusion(bf16[2816,2048]{1,0:T(8,128)(2,1)} %param.35, bf16[16,2048]{1,0:T(8,128)(2,1)S(1)} %multiply_convert_fusion.1, bf16[2816,2048]{1,0:T(8,128)(2,1)} %param.34, f32[16,2816]{1,0:T(8,128)S(1)} %fusion.44, f32[16]{0:T(128)S(1)} %fusion.39), kind=kOutput, calls=%fused_computation.17 | convolution fusion | flops 369414144 | bytes 23445568 | tf_op jit(solution)/shard_map/dot_general | solution.py:160
  194.8 103.2 %all-reduce.5.cloned.1.call-done = f32[16,2048]{1,0:T(8,128)} async-done(((f32[16,2048]{1,0:T(8,128)}), f32[16,2048]{1,0:T(8,128)}) %all-reduce.5.cloned.1.call-update) | async-done | bytes 131088 | tf_op jit(solution)/shard_map/psum | solution.py:161
  298.0 1.0 multiply_reduce_fusion
  299.0 5.6 %fusion.19 = f32[16,2000]{1,0:T(8,128)S(1)} fusion(bf16[2000,2048]{1,0:T(8,128)(2,1)} %param.37, f32[2048]{0:T(1024)S(1)} %convert_element_type.163, f32[16]{0:T(128)S(1)} %add_rsqrt_fusion, f32[16,2048]{1,0:T(8,128)} %all-reduce.5.cloned.1.call-done, f32[16,2048]{1,0:T(8,128)S(1)} %copy-done.1, bf16[1,16,2048]{2,1,0:T(8,128)(2,1)S(1)} %copy-done.2), kind=kOutput, calls=%fused_computation.35 | convolution fusion | flops 131268608 | bytes 8655936 | tf_op jit(solution)/shard_map/rd,vd->rv/dot_general | solution.py:165
  304.8 1.2 collective-permute-done
  306.0 0.7 multiply_add_fusion
  (56 shorter events, 1.5 us)
Async XLA Ops:
  6.5 56.5 %copy-start = (bf16[2048,8]{0,1:T(8,128)(2,1)S(1)}, bf16[2048,8]{0,1:T(8,128)(2,1)}, u32[]{:S(2)}) copy-start(bf16[2048,8]{0,1:T(8,128)(2,1)} %param.29) | copy-start | bytes 98308
  6.5 165.1 %copy-start.2 = (bf16[1,16,2048]{2,1,0:T(8,128)(2,1)S(1)}, bf16[1,16,2048]{2,1,0:T(8,128)(2,1)}, u32[]{:S(2)}) copy-start(bf16[1,16,2048]{2,1,0:T(8,128)(2,1)} %param.21) | copy-start | bytes 196612
  6.5 62.9 %copy-start.4 = (bf16[2048]{0:T(1024)(128)(2,1)S(1)}, bf16[2048]{0:T(1024)(128)(2,1)}, u32[]{:S(2)}) copy-start(bf16[2048]{0:T(1024)(128)(2,1)} %param.32) | copy-start | bytes 12292
  6.5 62.9 %copy-start.7 = (s32[4]{0:T(128)S(1)}, s32[4]{0:T(128)}, u32[]{:S(2)}) copy-start(s32[4]{0:T(128)} %param.38) | copy-start | bytes 52
  6.5 167.1 %copy-start.3 = (bf16[2048,8]{0,1:T(8,128)(2,1)S(1)}, bf16[2048,8]{0,1:T(8,128)(2,1)}, u32[]{:S(2)}) copy-start(bf16[2048,8]{0,1:T(8,128)(2,1)} %param.30) | copy-start | bytes 98308
  6.5 167.3 %copy-start.6 = (s32[16,2]{0,1:T(2,128)S(1)}, s32[16,2]{0,1:T(2,128)}, u32[]{:S(2)}) copy-start(s32[16,2]{0,1:T(2,128)} %param.28) | copy-start | bytes 388
  6.6 165.1 %all-reduce.3.cloned.1.call-start = ((), (), s32[]{:S(2)}) async-start(), calls=%async_computation | async-start | bytes 262144 | tf_op jit(solution)/shard_map/psum | solution.py:144
  69.4 228.6 %all-reduce.5.cloned.1.call-start = ((), (), s32[]{:S(2)}) async-start(), calls=%async_computation.1 | async-start | bytes 262144 | tf_op jit(solution)/shard_map/psum | solution.py:161
  181.3 13.5 %copy-start.5 = (bf16[2048]{0:T(1024)(128)(2,1)S(1)}, bf16[2048]{0:T(1024)(128)(2,1)}, u32[]{:S(2)}) copy-start(bf16[2048]{0:T(1024)(128)(2,1)} %param.36) | copy-start | bytes 12292
  181.3 13.5 %copy-start.8 = (s32[4]{0:T(128)S(1)}, s32[4]{0:T(128)}, u32[]{:S(2)}) copy-start(s32[4]{0:T(128)} %param.39) | copy-start | bytes 52
  181.3 116.7 %copy-start.1 = (f32[16,2048]{1,0:T(8,128)S(1)}, f32[16,2048]{1,0:T(8,128)}, u32[]{:S(2)}) copy-start(f32[16,2048]{1,0:T(8,128)} %all-reduce.3.cloned.1.call-done) | copy-start | bytes 393220
  304.7 1.3 collective-permute-start
Sparse Core Ops, SparseCore 0:
  69.5 102.1 all-reduce.2
  194.8 103.1 all-reduce.4
where the time goes:
time: 314 us
  waiting for transfers between devices  206 us (66%)
  blocking collectives  47.3 us (15%)
  matrix products  32.9 us (10%)
  between operations  13.7 us (4%)
  other arithmetic  9.26 us (3%)
  local copies, waits for them, and re-layouts  3.81 us (1%)
    psum x1, waiting for transfers between devices, local(): expert_out = lax.psum(expert_terms, ('blk', 'req'))  103 us
    psum x1, waiting for transfers between devices, local(): attention_proj = lax.psum(proj_terms, ('blk', 'req'))  102 us
    all_gather x3, blocking collectives, joined(): lax.all_gather(part.astype(kind), axis)  38.8 us
    dot_general x1, matrix products, local(): jnp.dot(expert_hidden, expert_down, preferred_element_type=jnp.float32)  13.3 us
    all_gather x1, blocking collectives, local(): lax.all_gather(attention_out, 'req', axis=0, tiled=True)  8.47 us
    dot_general x1, matrix products, local(): jnp.einsum('rd,fd->rf', expert_input, expert_gate, preferred_element_type...  7.36 us
  transfers between devices with their start and end apart: 3, of which 3 were waited for; matrix products, arithmetic and copies ran while one was open for 0% of the time, Pallas kernels for 0%

commit v1 on v0

--- a/solution.py
+++ b/solution.py
@@ -3,6 +3,8 @@
 import jax
 import jax.numpy as jnp
 from jax import lax
+from jax.experimental import pallas as pl
+from jax.experimental.pallas import tpu as pltpu
 from jax.sharding import PartitionSpec as P
 
 H = 16
@@ -181,6 +183,490 @@
     return unconditional + factor[:, None] * (conditional - unconditional)
 
 
+LANES = 128
+F32 = jnp.float32
+BF16 = jnp.bfloat16
+MESH = pl.DeviceIdType.MESH
+DEAD = -1e30
+
+
+def fits(mesh):
+    shape = dict(mesh.shape)
+    return shape["cfg"] == 2 and shape["blk"] == 4 and shape["req"] == 4
+
+
+def dot_nt(left, right):
+    return lax.dot_general(left, right, (((1,), (1,)), ((), ())), preferred_element_type=F32)
+
+
+def kernel_gates(logits, ids):
+    experts = lax.broadcasted_iota(jnp.int32, logits.shape, 1)
+    first = jnp.sum(jnp.where(experts == ids[:, 0:1], logits, 0.0), axis=1, keepdims=True)
+    second = jnp.sum(jnp.where(experts == ids[:, 1:2], logits, 0.0), axis=1, keepdims=True)
+    return jax.nn.sigmoid(first - second), jax.nn.sigmoid(second - first)
+
+
+def expert_share_of(logits, ids, expert):
+    first, second = kernel_gates(logits, ids)
+    return jnp.where(ids[:, 0:1] == expert, first, 0.0) + jnp.where(
+        ids[:, 1:2] == expert, second, 0.0
+    )
+
+
+def step_kernel(
+    n_blk,
+    n_req,
+    residual,
+    queries,
+    new_entries,
+    key_cache,
+    value_cache,
+    lengths,
+    att_ids,
+    att_ids_s,
+    exp_ids,
+    att_router,
+    exp_router,
+    w_proj,
+    gains,
+    w_gate,
+    w_up,
+    w_down,
+    w_head,
+    sizes,
+    guidance,
+    out,
+    keys,
+    values,
+    v_proj,
+    v_gate,
+    v_up,
+    v_down,
+    v_head,
+    send_a,
+    recv_a,
+    joint,
+    send_r,
+    recv_r,
+    send_g,
+    recv_g,
+    send_q,
+    recv_q,
+    send_f,
+    recv_f,
+    own_middle,
+    hidden,
+    kv_sem,
+    w_sem,
+    sems_s,
+    sems_r,
+    fin_s,
+    fin_r,
+):
+    n = n_blk * n_req
+    cfg = lax.axis_index("cfg")
+    blk = lax.axis_index("blk")
+    req = lax.axis_index("req")
+    me = blk * n_req + req
+    rows = queries.shape[1]
+    local_pos = key_cache.shape[2]
+    width = H * HD
+
+    barrier = pltpu.get_barrier_semaphore()
+
+    def greet(k, carry):
+        other = lax.rem(me + k, n)
+        for side in (0, 1):
+            pl.semaphore_signal(
+                barrier,
+                inc=1,
+                device_id=(side, other // n_req, lax.rem(other, n_req)),
+                device_id_type=MESH,
+            )
+        return carry
+
+    lax.fori_loop(1, n, greet, 0)
+    pl.semaphore_signal(barrier, inc=1, device_id=(1 - cfg, blk, req), device_id_type=MESH)
+
+    cache_copies = []
+    for r in range(rows):
+        for which, (source, target) in enumerate(((key_cache, keys), (value_cache, values))):
+            copy = pltpu.make_async_copy(
+                source.at[0, r], target.at[r, pl.ds(0, local_pos)], kv_sem.at[which, r]
+            )
+            copy.start()
+            cache_copies.append(copy)
+    weight_copies = []
+    for source, target in (
+        (w_proj, v_proj),
+        (w_gate, v_gate),
+        (w_up, v_up),
+        (w_down, v_down),
+        (w_head, v_head),
+    ):
+        copy = pltpu.make_async_copy(source, target, w_sem.at[len(weight_copies)])
+        copy.start()
+        weight_copies.append(copy)
+
+    def send(source_of, target, phase, k):
+        other = lax.rem(me + k, n)
+        return pltpu.make_async_remote_copy(
+            src_ref=source_of(other),
+            dst_ref=target.at[me],
+            send_sem=sems_s.at[phase, other],
+            recv_sem=sems_r.at[phase, me],
+            device_id=(cfg, other // n_req, lax.rem(other, n_req)),
+            device_id_type=MESH,
+        )
+
+    def start_all(source_of, target, phase):
+        def go(k, carry):
+            send(source_of, target, phase, k).start()
+            return carry
+
+        lax.fori_loop(1, n, go, 0)
+
+    def finish_all(source_of, target, phase):
+        def go(k, carry):
+            source = lax.rem(me + n - k, n)
+            pltpu.make_async_remote_copy(
+                src_ref=source_of(me),
+                dst_ref=target.at[source],
+                send_sem=sems_s.at[phase, source],
+                recv_sem=sems_r.at[phase, source],
+                device_id=(cfg, source // n_req, lax.rem(source, n_req)),
+                device_id_type=MESH,
+            ).wait()
+            return carry
+
+        lax.fori_loop(1, n, go, 0)
+
+    extra = keys.shape[1] - local_pos
+    head_of_row = lax.rem(lax.broadcasted_iota(jnp.int32, (TOPK * H, 1), 0), H)
+    head_of_column = lax.broadcasted_iota(jnp.int32, (TOPK * H, width), 1) // HD
+    own_head = head_of_row == head_of_column
+    place = lax.broadcasted_iota(jnp.int32, (1, keys.shape[1]), 1)
+    new_row = lax.broadcasted_iota(jnp.int32, (extra, 1), 0) == 0
+    query_all = queries[0].astype(F32)
+    outs = []
+    tops = []
+    for r in range(rows):
+        entries = new_entries[0, r].astype(F32)
+        keys[r, pl.ds(local_pos, extra)] = jnp.where(new_row, entries[0:1], 0.0).astype(BF16)
+        values[r, pl.ds(local_pos, extra)] = jnp.where(new_row, entries[1:2], 0.0).astype(BF16)
+        cache_copies[2 * r].wait()
+        cache_copies[2 * r + 1].wait()
+        spread = jnp.concatenate(
+            [
+                jnp.broadcast_to(query_all[r : r + 1, k * width : (k + 1) * width], (H, width))
+                for k in range(TOPK)
+            ],
+            axis=0,
+        )
+        spread = jnp.where(own_head, spread, 0.0).astype(BF16)
+        scores = dot_nt(spread, keys[r]) * (1.0 / math.sqrt(HD))
+        cached = (place < local_pos) & (place + blk * local_pos < lengths[0, r])
+        live = cached | ((place == local_pos) & (blk == 0))
+        top = jnp.max(jnp.where(live, scores, DEAD), axis=1, keepdims=True)
+        weights = jnp.where(live, jnp.exp(scores - top), 0.0)
+        total = jnp.sum(weights, axis=1, keepdims=True)
+        wide = jnp.dot(weights.astype(BF16), values[r], preferred_element_type=F32)
+        acc = jnp.zeros((TOPK * H, HD), F32)
+        for h in range(H):
+            acc = acc + jnp.where(head_of_row == h, wide[:, h * HD : (h + 1) * HD], 0.0)
+        alive = total > 0.0
+        safe = jnp.where(alive, total, 1.0)
+        outs.append(acc / safe)
+        tops.append(jnp.where(alive, top + jnp.log(safe), DEAD))
+
+    lane = lax.broadcasted_iota(jnp.int32, (2 * H, LANES), 1)
+    half = H // 2
+    for e in range(n // 2):
+        picked = []
+        levels = []
+        for r in range(rows):
+            first = jnp.where(att_ids_s[req * rows + r, 0] == e, 1.0, 0.0)
+            second = jnp.where(att_ids_s[req * rows + r, 1] == e, 1.0, 0.0)
+            picked.append(first * outs[r][:H] + second * outs[r][H:])
+            levels.append(first * tops[r][:H] + second * tops[r][H:])
+        for side in range(2):
+            cut = slice(side * half, (side + 1) * half)
+            block = jnp.concatenate([part[cut] for part in picked], axis=0)
+            level = jnp.concatenate([part[cut] for part in levels], axis=0)
+            high = level.astype(BF16).astype(F32)
+            mid = (level - high).astype(BF16).astype(F32)
+            low = level - high - mid
+            parts = jnp.where(
+                lax.rem(lane, 3) == 0, high, jnp.where(lax.rem(lane, 3) == 1, mid, low)
+            )
+            stats = jnp.where(
+                lane[:H] < 3, parts[:H], jnp.where(lane[:H] < 6, parts[H:], 0.0)
+            )
+            send_a[2 * e + side] = jnp.concatenate([block, stats], axis=0).astype(BF16)
+
+    pl.semaphore_wait(barrier, 2 * n - 1)
+    start_all(lambda other: send_a.at[other], recv_a, 0)
+    recv_a[me] = send_a[me]
+
+    inputs = residual[0].astype(F32)
+    normed = rms_scale(inputs).astype(BF16)
+    att_logits = jnp.dot(normed, att_router[...], preferred_element_type=F32)
+    att_share = expert_share_of(att_logits, att_ids[...], me // 2)
+    weight_copies[0].wait()
+    finish_all(lambda other: send_a.at[other], recv_a, 0)
+
+    small = lax.broadcasted_iota(jnp.int32, (H, LANES), 1)
+    for q in range(n_req):
+        blocks = []
+        levels = []
+        for b in range(n_blk):
+            message = recv_a[b * n_req + q].astype(F32)
+            stats = message[2 * H :]
+            upper = jnp.sum(jnp.where(small < 3, stats, 0.0), axis=1, keepdims=True)
+            lower = jnp.sum(
+                jnp.where((small >= 3) & (small < 6), stats, 0.0), axis=1, keepdims=True
+            )
+            levels.append(jnp.concatenate([upper, lower], axis=0))
+            blocks.append(message[: 2 * H])
+        peak = levels[0]
+        for b in range(1, n_blk):
+            peak = jnp.maximum(peak, levels[b])
+        total = jnp.zeros_like(peak)
+        mixed = jnp.zeros_like(blocks[0])
+        for b in range(n_blk):
+            weight = jnp.exp(levels[b] - peak)
+            total = total + weight
+            mixed = mixed + weight * blocks[b]
+        joint[pl.ds(q * 2 * H, 2 * H)] = (mixed / total).astype(BF16).astype(F32)
+    gathered = jnp.concatenate(
+        [joint[pl.ds(h, n_req * rows, stride=half), :] for h in range(half)], axis=1
+    )
+    selected = (gathered * att_share).astype(BF16)
+
+    def scatter(product_of, send_buf):
+        for t in range(4):
+            part = product_of(t)
+            for j in range(4):
+                send_buf[4 * t + j] = part[:, j * LANES : (j + 1) * LANES].astype(BF16)
+
+    def summed(buf):
+        total = buf[0].astype(F32)
+        for k in range(1, n):
+            total = total + buf[k].astype(F32)
+        return total
+
+    def whole(buf):
+        return jnp.concatenate([buf[k].astype(F32) for k in range(n)], axis=1)
+
+    scatter(
+        lambda t: jnp.dot(
+            selected, v_proj[:, t * 512 : (t + 1) * 512], preferred_element_type=F32
+        ),
+        send_r,
+    )
+    start_all(lambda other: send_r.at[other], recv_r, 1)
+    recv_r[me] = send_r[me]
+    finish_all(lambda other: send_r.at[other], recv_r, 1)
+    own_column = pl.multiple_of(me * LANES, LANES)
+    own_middle[...] = summed(recv_r) + residual[0, :, pl.ds(own_column, LANES)].astype(F32)
+    send_g[...] = own_middle[...].astype(BF16)
+    start_all(lambda other: send_g, recv_g, 2)
+    recv_g[me] = send_g[...]
+    weight_copies[1].wait()
+    weight_copies[2].wait()
+    finish_all(lambda other: send_g, recv_g, 2)
+
+    expert_input = (rms_scale(whole(recv_g)) * gains[0:1, :]).astype(BF16)
+    exp_logits = jnp.dot(expert_input, exp_router[...], preferred_element_type=F32)
+    share = expert_share_of(exp_logits, exp_ids[...], me * v_gate.shape[0] // FF)
+
+    def feed(t, carry):
+        start = pl.multiple_of(t * 256, 256)
+        gate_values = dot_nt(expert_input, v_gate[pl.ds(start, 256), :])
+        up_values = dot_nt(expert_input, v_up[pl.ds(start, 256), :])
+        hidden[t] = (jax.nn.silu(gate_values) * up_values * share).astype(BF16)
+        return carry
+
+    tiles = v_gate.shape[0] // 256
+    lax.fori_loop(0, tiles, feed, 0)
+    weight_copies[3].wait()
+    all_hidden = jnp.concatenate([hidden[t] for t in range(tiles)], axis=1)
+    scatter(
+        lambda t: jnp.dot(
+            all_hidden, v_down[:, t * 512 : (t + 1) * 512], preferred_element_type=F32
+        ),
+        send_q,
+    )
+    start_all(lambda other: send_q.at[other], recv_q, 3)
+    recv_q[me] = send_q[me]
+    finish_all(lambda other: send_q.at[other], recv_q, 3)
+    send_f[...] = (own_middle[...] + summed(recv_q)).astype(BF16)
+
+    def final_copy(k, side, other, source_side, source):
+        return pltpu.make_async_remote_copy(
+            src_ref=send_f,
+            dst_ref=recv_f.at[source_side, source],
+            send_sem=fin_s.at[lax.rem(side + 2 - source_side, 2), k],
+            recv_sem=fin_r.at[source_side, source],
+            device_id=(side, other // n_req, lax.rem(other, n_req)),
+            device_id_type=MESH,
+        )
+
+    def final_send(k, carry):
+        other = lax.rem(me + k, n)
+        final_copy(k, cfg, other, cfg, me).start()
+        final_copy(k, 1 - cfg, other, cfg, me).start()
+        return carry
+
+    def final_wait(k, carry):
+        source = lax.rem(me + n - k, n)
+        for side in (0, 1):
+            pltpu.make_async_remote_copy(
+                src_ref=send_f,
+                dst_ref=recv_f.at[lax.rem(cfg + side, 2), source],
+                send_sem=fin_s.at[side, k],
+                recv_sem=fin_r.at[lax.rem(cfg + side, 2), source],
+                device_id=(lax.rem(cfg + side, 2), source // n_req, lax.rem(source, n_req)),
+                device_id_type=MESH,
+            ).wait()
+        return carry
+
+    final_copy(0, 1 - cfg, me, cfg, me).start()
+    lax.fori_loop(1, n, final_send, 0)
+    recv_f[cfg, me] = send_f[...]
+    weight_copies[4].wait()
+    pltpu.make_async_remote_copy(
+        src_ref=send_f,
+        dst_ref=recv_f.at[1 - cfg, me],
+        send_sem=fin_s.at[1, 0],
+        recv_sem=fin_r.at[1 - cfg, me],
+        device_id=(1 - cfg, blk, req),
+        device_id_type=MESH,
+    ).wait()
+    lax.fori_loop(1, n, final_wait, 0)
+
+    guided_rows = out.shape[0]
+    mine = []
+    for stream in (0, 1):
+        both = whole(recv_f.at[stream])
+        mine.append(jnp.where(cfg == 0, both[:guided_rows], both[guided_rows:]))
+    final_input = (rms_scale(jnp.concatenate(mine, axis=0)) * gains[1:2, :]).astype(BF16)
+    request = cfg * guided_rows + lax.broadcasted_iota(jnp.int32, (guided_rows, LANES), 0)
+    tenant = jnp.zeros_like(request)
+    end = 0
+    for t in range(sizes.shape[0]):
+        end = end + sizes[t]
+        tenant = tenant + jnp.where(request >= end, 1, 0)
+    guide = jnp.zeros_like(request)
+    for t in range(sizes.shape[0]):
+        guide = guide + jnp.where(tenant == t, guidance[t], 0)
+    factor = guide.astype(F32)[:, 0:1] / 4.0
+    words = v_head.shape[0]
+    for first in range(0, words, 512):
+        last = min(first + 512, words)
+        logits = dot_nt(final_input, v_head[first:last, :])
+        conditional, unconditional = logits[:guided_rows], logits[guided_rows:]
+        out[:, first:last] = unconditional + factor * (conditional - unconditional)
+
+
+def fused(
+    residual,
+    queries,
+    new_entries,
+    key_cache,
+    value_cache,
+    lengths,
+    attention_ids,
+    expert_ids,
+    attention_router,
+    expert_router,
+    attention_output,
+    expert_gain,
+    expert_gate,
+    expert_up,
+    expert_down,
+    final_gain,
+    unembedding,
+    tenant_sizes,
+    guidance,
+):
+    n_blk, n_req = lax.axis_size("blk"), lax.axis_size("req")
+    n = n_blk * n_req
+    requests = residual.shape[1]
+    rows = queries.shape[1]
+    positions = key_cache.shape[2] + 16
+    width = H * HD
+    vmem = pl.BlockSpec(memory_space=pltpu.VMEM)
+    smem = pl.BlockSpec(memory_space=pltpu.SMEM)
+    hbm = pl.BlockSpec(memory_space=pl.ANY)
+    gains = jnp.stack([expert_gain, final_gain]).astype(F32)
+    block = (requests, LANES)
+    weights = attention_output.size + 3 * expert_gate.size + unembedding.size
+    return pl.pallas_call(
+        lambda *refs: step_kernel(n_blk, n_req, *refs),
+        out_shape=jax.ShapeDtypeStruct((requests // 2, unembedding.shape[0]), F32),
+        in_specs=[
+            vmem, vmem, vmem, hbm, hbm, smem, vmem, smem, vmem, vmem, vmem,
+            hbm, vmem, hbm, hbm, hbm, hbm, smem, smem,
+        ],
+        out_specs=vmem,
+        scratch_shapes=[
+            pltpu.VMEM((rows, positions, width), BF16),
+            pltpu.VMEM((rows, positions, width), BF16),
+            pltpu.VMEM(attention_output.shape, BF16),
+            pltpu.VMEM(expert_gate.shape, BF16),
+            pltpu.VMEM(expert_up.shape, BF16),
+            pltpu.VMEM(expert_down.shape, BF16),
+            pltpu.VMEM(unembedding.shape, BF16),
+            pltpu.VMEM((n, 3 * H, LANES), BF16),
+            pltpu.VMEM((n, 3 * H, LANES), BF16),
+            pltpu.VMEM((requests * H // 2, LANES), F32),
+            pltpu.VMEM((n, *block), BF16),
+            pltpu.VMEM((n, *block), BF16),
+            pltpu.VMEM(block, BF16),
+            pltpu.VMEM((n, *block), BF16),
+            pltpu.VMEM((n, *block), BF16),
+            pltpu.VMEM((n, *block), BF16),
+            pltpu.VMEM(block, BF16),
+            pltpu.VMEM((2, n, *block), BF16),
+            pltpu.VMEM(block, F32),
+            pltpu.VMEM((expert_gate.shape[0] // 256, requests, 256), BF16),
+            pltpu.SemaphoreType.DMA((2, rows)),
+            pltpu.SemaphoreType.DMA((5,)),
+            pltpu.SemaphoreType.DMA((4, n)),
+            pltpu.SemaphoreType.DMA((4, n)),
+            pltpu.SemaphoreType.DMA((2, n)),
+            pltpu.SemaphoreType.DMA((2, n)),
+        ],
+        compiler_params=pltpu.CompilerParams(
+            collective_id=0, has_side_effects=True, vmem_limit_bytes=60 * 2**20
+        ),
+        cost_estimate=pl.CostEstimate(
+            flops=2 * requests * weights, bytes_accessed=2 * weights, transcendentals=0
+        ),
+    )(
+        residual,
+        queries,
+        new_entries,
+        key_cache,
+        value_cache,
+        lengths,
+        attention_ids,
+        attention_ids,
+        expert_ids,
+        attention_router,
+        expert_router,
+        attention_output,
+        gains,
+        expert_gate,
+        expert_up,
+        expert_down,
+        unembedding,
+        tenant_sizes,
+        guidance,
+    )
+
+
 def solution(mesh):
     placed = (
         P("cfg", None, None),
@@ -203,6 +689,7 @@
         P(),
         P(),
     )
+    body = fused if fits(mesh) else local
     return jax.shard_map(
-        local, mesh=mesh, in_specs=placed, out_specs=P("cfg", ("blk", "req")), check_vma=False
-    )
+        body, mesh=mesh, in_specs=placed, out_specs=P("cfg", ("blk", "req")), check_vma=False
+    )

time: 314 us -> 65.8 us (0.21)
  waiting for transfers between devices: 206 us -> 0 us
  Pallas kernels: 0 us -> 55.6 us
  blocking collectives: 47.3 us -> 0 us
  matrix products: 32.9 us -> 0 us
  between operations: 13.7 us -> 0.01 us
  other arithmetic: 9.26 us -> 0.63 us
  local copies, waits for them, and re-layouts: 3.81 us -> 9.1 us
    psum x2 -> x0, waiting for transfers between devices: 205 us -> none  [the longest x1 103 us: local(): expert_out = lax.psum(expert_terms, ('blk', 'req'))]
    pallas_call x0 -> x1, Pallas kernels: none -> 55.6 us  [fused(): pl.pallas_call(lambda *refs: step_kernel(n_blk, n_req, *refs), out_shape=...]
    all_gather x4 -> x0, blocking collectives: 47.3 us -> none  [the longest x3 38.8 us: joined(): lax.all_gather(part.astype(kind), axis)]
    dot_general x9 -> x0, matrix products: 32.9 us -> none  [the longest x1 13.3 us: local(): jnp.dot(expert_hidden, expert_down, preferred_element_type=jnp.float32)]
    reduce_sum x10 -> x0, other arithmetic: 4.5 us -> none  [the longest x3 3.04 us: rms_scale(): jnp.mean(values * values, axis=-1, keepdims=True) + EPS]
    unnamed x21 -> x5, local copies, waits for them, and re-layouts: 3.38 us -> 7.72 us
  transfers between devices with their start and end apart: 3 -> 0, of which waited for: 3 -> 0; matrix products, arithmetic and copies ran while one was open for 0% -> 0% of each run, Pallas kernels for 0% -> 0%
where the time goes in v1:
time: 65.8 us; the launch traced here: 65.4 us
  Pallas kernels  55.6 us (84%)
  local copies, waits for them, and re-layouts  9.1 us (14%)
    pallas_call x1, Pallas kernels, fused(): pl.pallas_call(lambda *refs: step_kernel(n_blk, n_req, *refs), out_shape=...  55.6 us
    unnamed x5, local copies, waits for them, and re-layouts  7.72 us
    another operation x2, local copies, waits for them, and re-layouts, fused(): gains = jnp.stack([expert_gain, final_gain]).astype(F32)  1.39 us

profile of v1, /device:TPU:0, one launch (start us, length us, event | category | flops | bytes accessed | tf_op | source)
XLA Modules:
  0.0 65.4 jit_solution(2223982940322172853)
XLA Ops:
  0.0 1.4 %copy.20.refs_6_.refs_7_ = s32[16,2]{1,0:T(8,128)} copy(s32[16,2]{0,1:T(2,128)} %param.25) | data formatting | bytes 256 | tf_op args[6]
  1.4 1.3 %copy.22.refs_8_ = s32[16,2]{1,0:T(8,128)} copy(s32[16,2]{0,1:T(2,128)} %param.26) | data formatting | bytes 256 | tf_op args[7]
  2.7 0.7 %stack.9 = bf16[1,2048]{1,0:T(2,128)(2,1)S(1)} reshape(bf16[2048]{0:T(1024)(128)(2,1)} %param.30) | data formatting | bytes 8192 | tf_op jit(solution)/shard_map/stack | solution.py:602
  3.4 0.7 %stack.10 = bf16[1,2048]{1,0:T(2,128)(2,1)S(1)} reshape(bf16[2048]{0:T(1024)(128)(2,1)} %param.34) | data formatting | bytes 8192 | tf_op jit(solution)/shard_map/stack | solution.py:602
  4.1 0.6 maximum_convert_fusion.refs_12_
  4.7 1.8 %copy.23.refs_9_ = bf16[2048,8]{1,0:T(8,128)(2,1)} copy(bf16[2048,8]{0,1:T(8,128)(2,1)} %param.27) | data formatting | bytes 65536 | tf_op args[8]
  6.5 1.8 %copy.24.refs_10_ = bf16[2048,8]{1,0:T(8,128)(2,1)} copy(bf16[2048,8]{0,1:T(8,128)(2,1)} %param.28) | data formatting | bytes 65536 | tf_op args[9]
  8.3 55.6 %shard_map.181 = f32[8,2000]{1,0:T(8,128)} custom-call(bf16[1,16,2048]{2,1,0:T(8,128)(2,1)} %refs_0_.1, bf16[1,4,4096]{2,1,0:T(4,128)(2,1)} %refs_1_.1, bf16[1,4,2,2048]{3,2,1,0:T(2,128)(2,1)} %refs_2_.1, bf16[1,4,48,2048]{3,2,1,0:T(8,128)(2,1)} %refs_3_.1, bf16[1,4,48,2048]{3,2,1,0:T(8,128)(2,1)} %refs_4_.1, s32[1,4]{1,0:T(1,128)} %refs_5_.1, ...), custom_call_target="tpu_custom_call" | custom-call | flops 751828992 | bytes 46989312 | tf_op jit(solution)/shard_map/pallas_call | solution.py:605
  63.9 1.5 %copy.26 = f32[8,2000]{1,0:T(8,128)} copy(f32[8,2000]{1,0:T(8,128)} %shard_map.181) | data formatting | bytes 128000

commit v2 on v1

--- a/solution.py
+++ b/solution.py
@@ -199,18 +199,21 @@
     return lax.dot_general(left, right, (((1,), (1,)), ((), ())), preferred_element_type=F32)
 
 
-def kernel_gates(logits, ids):
-    experts = lax.broadcasted_iota(jnp.int32, logits.shape, 1)
-    first = jnp.sum(jnp.where(experts == ids[:, 0:1], logits, 0.0), axis=1, keepdims=True)
-    second = jnp.sum(jnp.where(experts == ids[:, 1:2], logits, 0.0), axis=1, keepdims=True)
-    return jax.nn.sigmoid(first - second), jax.nn.sigmoid(second - first)
-
-
 def expert_share_of(logits, ids, expert):
-    first, second = kernel_gates(logits, ids)
-    return jnp.where(ids[:, 0:1] == expert, first, 0.0) + jnp.where(
-        ids[:, 1:2] == expert, second, 0.0
-    )
+    experts = lax.broadcasted_iota(jnp.int32, logits.shape, 0)
+    first = jnp.sum(jnp.where(experts == ids[0:1], logits, 0.0), axis=0, keepdims=True)
+    second = jnp.sum(jnp.where(experts == ids[1:2], logits, 0.0), axis=0, keepdims=True)
+    return jnp.where(ids[0:1] == expert, jax.nn.sigmoid(first - second), 0.0) + jnp.where(
+        ids[1:2] == expert, jax.nn.sigmoid(second - first), 0.0
+    )
+
+
+def as_column(row):
+    extent = row.shape[1]
+    diagonal = lax.broadcasted_iota(jnp.int32, (extent, extent), 0) == lax.broadcasted_iota(
+        jnp.int32, (extent, extent), 1
+    )
+    return jnp.sum(jnp.where(diagonal, row, 0.0), axis=1, keepdims=True)
 
 
 def step_kernel(
@@ -228,7 +231,8 @@
     att_router,
     exp_router,
     w_proj,
-    gains,
+    gain_in,
+    gain_out,
     w_gate,
     w_up,
     w_down,
@@ -255,13 +259,10 @@
     send_f,
     recv_f,
     own_middle,
-    hidden,
     kv_sem,
     w_sem,
     sems_s,
     sems_r,
-    fin_s,
-    fin_r,
 ):
     n = n_blk * n_req
     cfg = lax.axis_index("cfg")
@@ -308,38 +309,30 @@
         copy.start()
         weight_copies.append(copy)
 
-    def send(source_of, target, phase, k):
-        other = lax.rem(me + k, n)
+    def start_all(source_of, target, phase):
+        def go(k, carry):
+            other = lax.rem(me + k, n)
+            pltpu.make_async_remote_copy(
+                src_ref=source_of(other),
+                dst_ref=target.at[me],
+                send_sem=sems_s.at[phase],
+                recv_sem=sems_r.at[phase],
+                device_id=(cfg, other // n_req, lax.rem(other, n_req)),
+                device_id_type=MESH,
+            ).start()
+            return carry
+
+        lax.fori_loop(1, n, go, 0, unroll=True)
+
+    def all_blocks(target, phase):
         return pltpu.make_async_remote_copy(
-            src_ref=source_of(other),
-            dst_ref=target.at[me],
-            send_sem=sems_s.at[phase, other],
-            recv_sem=sems_r.at[phase, me],
-            device_id=(cfg, other // n_req, lax.rem(other, n_req)),
+            src_ref=target.at[pl.ds(0, n - 1)],
+            dst_ref=target.at[pl.ds(0, n - 1)],
+            send_sem=sems_s.at[phase],
+            recv_sem=sems_r.at[phase],
+            device_id=(1 - cfg, blk, req),
             device_id_type=MESH,
         )
-
-    def start_all(source_of, target, phase):
-        def go(k, carry):
-            send(source_of, target, phase, k).start()
-            return carry
-
-        lax.fori_loop(1, n, go, 0)
-
-    def finish_all(source_of, target, phase):
-        def go(k, carry):
-            source = lax.rem(me + n - k, n)
-            pltpu.make_async_remote_copy(
-                src_ref=source_of(me),
-                dst_ref=target.at[source],
-                send_sem=sems_s.at[phase, source],
-                recv_sem=sems_r.at[phase, source],
-                device_id=(cfg, source // n_req, lax.rem(source, n_req)),
-                device_id_type=MESH,
-            ).wait()
-            return carry
-
-        lax.fori_loop(1, n, go, 0)
 
     extra = keys.shape[1] - local_pos
     head_of_row = lax.rem(lax.broadcasted_iota(jnp.int32, (TOPK * H, 1), 0), H)
@@ -350,12 +343,12 @@
     query_all = queries[0].astype(F32)
     outs = []
     tops = []
+    for copy in cache_copies:
+        copy.wait()
     for r in range(rows):
         entries = new_entries[0, r].astype(F32)
         keys[r, pl.ds(local_pos, extra)] = jnp.where(new_row, entries[0:1], 0.0).astype(BF16)
         values[r, pl.ds(local_pos, extra)] = jnp.where(new_row, entries[1:2], 0.0).astype(BF16)
-        cache_copies[2 * r].wait()
-        cache_copies[2 * r + 1].wait()
         spread = jnp.concatenate(
             [
                 jnp.broadcast_to(query_all[r : r + 1, k * width : (k + 1) * width], (H, width))
@@ -385,8 +378,8 @@
         picked = []
         levels = []
         for r in range(rows):
-            first = jnp.where(att_ids_s[req * rows + r, 0] == e, 1.0, 0.0)
-            second = jnp.where(att_ids_s[req * rows + r, 1] == e, 1.0, 0.0)
+            first = jnp.where(att_ids_s[0, req * rows + r] == e, 1.0, 0.0)
+            second = jnp.where(att_ids_s[1, req * rows + r] == e, 1.0, 0.0)
             picked.append(first * outs[r][:H] + second * outs[r][H:])
             levels.append(first * tops[r][:H] + second * tops[r][H:])
         for side in range(2):
@@ -410,10 +403,10 @@
 
     inputs = residual[0].astype(F32)
     normed = rms_scale(inputs).astype(BF16)
-    att_logits = jnp.dot(normed, att_router[...], preferred_element_type=F32)
-    att_share = expert_share_of(att_logits, att_ids[...], me // 2)
+    att_logits = dot_nt(att_router[...], normed)
+    att_share = as_column(expert_share_of(att_logits, att_ids[...], me // 2))
     weight_copies[0].wait()
-    finish_all(lambda other: send_a.at[other], recv_a, 0)
+    all_blocks(recv_a, 0).wait_recv()
 
     small = lax.broadcasted_iota(jnp.int32, (H, LANES), 1)
     for q in range(n_req):
@@ -458,6 +451,10 @@
     def whole(buf):
         return jnp.concatenate([buf[k].astype(F32) for k in range(n)], axis=1)
 
+    def gain_row(gain):
+        wide = gain[...].astype(F32)
+        return jnp.concatenate([wide[k : k + 1] for k in range(n)], axis=1)
+
     scatter(
         lambda t: jnp.dot(
             selected, v_proj[:, t * 512 : (t + 1) * 512], preferred_element_type=F32
@@ -466,7 +463,7 @@
     )
     start_all(lambda other: send_r.at[other], recv_r, 1)
     recv_r[me] = send_r[me]
-    finish_all(lambda other: send_r.at[other], recv_r, 1)
+    all_blocks(recv_r, 1).wait_recv()
     own_column = pl.multiple_of(me * LANES, LANES)
     own_middle[...] = summed(recv_r) + residual[0, :, pl.ds(own_column, LANES)].astype(F32)
     send_g[...] = own_middle[...].astype(BF16)
@@ -474,23 +471,21 @@
     recv_g[me] = send_g[...]
     weight_copies[1].wait()
     weight_copies[2].wait()
-    finish_all(lambda other: send_g, recv_g, 2)
-
-    expert_input = (rms_scale(whole(recv_g)) * gains[0:1, :]).astype(BF16)
-    exp_logits = jnp.dot(expert_input, exp_router[...], preferred_element_type=F32)
-    share = expert_share_of(exp_logits, exp_ids[...], me * v_gate.shape[0] // FF)
-
-    def feed(t, carry):
-        start = pl.multiple_of(t * 256, 256)
-        gate_values = dot_nt(expert_input, v_gate[pl.ds(start, 256), :])
-        up_values = dot_nt(expert_input, v_up[pl.ds(start, 256), :])
-        hidden[t] = (jax.nn.silu(gate_values) * up_values * share).astype(BF16)
-        return carry
-
-    tiles = v_gate.shape[0] // 256
-    lax.fori_loop(0, tiles, feed, 0)
+    all_blocks(recv_g, 2).wait_recv()
+
+    expert_input = (rms_scale(whole(recv_g)) * gain_row(gain_in)).astype(BF16)
+    share = expert_share_of(
+        dot_nt(exp_router[...], expert_input), exp_ids[...], me * v_gate.shape[0] // FF
+    )
+    tile = v_gate.shape[0] // 2
+    pieces = []
+    for t in range(2):
+        gate_values = dot_nt(v_gate[t * tile : (t + 1) * tile, :], expert_input)
+        up_values = dot_nt(v_up[t * tile : (t + 1) * tile, :], expert_input)
+        part = jax.nn.silu(gate_values) * up_values * share
+        pieces.append(jnp.transpose(part).astype(BF16))
     weight_copies[3].wait()
-    all_hidden = jnp.concatenate([hidden[t] for t in range(tiles)], axis=1)
+    all_hidden = jnp.concatenate(pieces, axis=1)
     scatter(
         lambda t: jnp.dot(
             all_hidden, v_down[:, t * 512 : (t + 1) * 512], preferred_element_type=F32
@@ -499,58 +494,49 @@
     )
     start_all(lambda other: send_q.at[other], recv_q, 3)
     recv_q[me] = send_q[me]
-    finish_all(lambda other: send_q.at[other], recv_q, 3)
+    all_blocks(recv_q, 3).wait_recv()
     send_f[...] = (own_middle[...] + summed(recv_q)).astype(BF16)
 
-    def final_copy(k, side, other, source_side, source):
-        return pltpu.make_async_remote_copy(
+    def final_send(away, other):
+        side = 1 - cfg if away else cfg
+        pltpu.make_async_remote_copy(
             src_ref=send_f,
-            dst_ref=recv_f.at[source_side, source],
-            send_sem=fin_s.at[lax.rem(side + 2 - source_side, 2), k],
-            recv_sem=fin_r.at[source_side, source],
+            dst_ref=recv_f.at[cfg, me],
+            send_sem=sems_s.at[4 + away],
+            recv_sem=sems_r.at[4 + away],
             device_id=(side, other // n_req, lax.rem(other, n_req)),
             device_id_type=MESH,
-        )
-
-    def final_send(k, carry):
+        ).start()
+
+    def final_step(k, carry):
         other = lax.rem(me + k, n)
-        final_copy(k, cfg, other, cfg, me).start()
-        final_copy(k, 1 - cfg, other, cfg, me).start()
+        final_send(0, other)
+        final_send(1, other)
         return carry
 
-    def final_wait(k, carry):
-        source = lax.rem(me + n - k, n)
-        for side in (0, 1):
-            pltpu.make_async_remote_copy(
-                src_ref=send_f,
-                dst_ref=recv_f.at[lax.rem(cfg + side, 2), source],
-                send_sem=fin_s.at[side, k],
-                recv_sem=fin_r.at[lax.rem(cfg + side, 2), source],
-                device_id=(lax.rem(cfg + side, 2), source // n_req, lax.rem(source, n_req)),
-                device_id_type=MESH,
-            ).wait()
-        return carry
-
-    final_copy(0, 1 - cfg, me, cfg, me).start()
-    lax.fori_loop(1, n, final_send, 0)
+    lax.fori_loop(1, n, final_step, 0, unroll=True)
+    final_send(1, me)
     recv_f[cfg, me] = send_f[...]
     weight_copies[4].wait()
-    pltpu.make_async_remote_copy(
-        src_ref=send_f,
-        dst_ref=recv_f.at[1 - cfg, me],
-        send_sem=fin_s.at[1, 0],
-        recv_sem=fin_r.at[1 - cfg, me],
-        device_id=(1 - cfg, blk, req),
-        device_id_type=MESH,
-    ).wait()
-    lax.fori_loop(1, n, final_wait, 0)
+    for away in (0, 1):
+        target = recv_f.at[0, pl.ds(0, n - 1 + away)]
+        pltpu.make_async_remote_copy(
+            src_ref=target,
+            dst_ref=target,
+            send_sem=sems_s.at[4 + away],
+            recv_sem=sems_r.at[4 + away],
+            device_id=(1 - cfg, blk, req),
+            device_id_type=MESH,
+        ).wait()
+    for phase, target in enumerate((recv_a, recv_r, recv_g, recv_q)):
+        all_blocks(target, phase).wait_send()
 
     guided_rows = out.shape[0]
     mine = []
     for stream in (0, 1):
         both = whole(recv_f.at[stream])
         mine.append(jnp.where(cfg == 0, both[:guided_rows], both[guided_rows:]))
-    final_input = (rms_scale(jnp.concatenate(mine, axis=0)) * gains[1:2, :]).astype(BF16)
+    final_input = (rms_scale(jnp.concatenate(mine, axis=0)) * gain_row(gain_out)).astype(BF16)
     request = cfg * guided_rows + lax.broadcasted_iota(jnp.int32, (guided_rows, LANES), 0)
     tenant = jnp.zeros_like(request)
     end = 0
@@ -562,9 +548,9 @@
         guide = guide + jnp.where(tenant == t, guidance[t], 0)
     factor = guide.astype(F32)[:, 0:1] / 4.0
     words = v_head.shape[0]
-    for first in range(0, words, 512):
-        last = min(first + 512, words)
-        logits = dot_nt(final_input, v_head[first:last, :])
+    for first in range(0, words, 1024):
+        last = min(first + 1024, words)
+        logits = jnp.transpose(dot_nt(v_head[first:last, :], final_input))
         conditional, unconditional = logits[:guided_rows], logits[guided_rows:]
         out[:, first:last] = unconditional + factor * (conditional - unconditional)
 
@@ -599,7 +585,6 @@
     vmem = pl.BlockSpec(memory_space=pltpu.VMEM)
     smem = pl.BlockSpec(memory_space=pltpu.SMEM)
     hbm = pl.BlockSpec(memory_space=pl.ANY)
-    gains = jnp.stack([expert_gain, final_gain]).astype(F32)
     block = (requests, LANES)
     weights = attention_output.size + 3 * expert_gate.size + unembedding.size
     return pl.pallas_call(
@@ -607,7 +592,7 @@
         out_shape=jax.ShapeDtypeStruct((requests // 2, unembedding.shape[0]), F32),
         in_specs=[
             vmem, vmem, vmem, hbm, hbm, smem, vmem, smem, vmem, vmem, vmem,
-            hbm, vmem, hbm, hbm, hbm, hbm, smem, smem,
+            hbm, vmem, vmem, hbm, hbm, hbm, hbm, smem, smem,
         ],
         out_specs=vmem,
         scratch_shapes=[
@@ -630,13 +615,10 @@
             pltpu.VMEM(block, BF16),
             pltpu.VMEM((2, n, *block), BF16),
             pltpu.VMEM(block, F32),
-            pltpu.VMEM((expert_gate.shape[0] // 256, requests, 256), BF16),
             pltpu.SemaphoreType.DMA((2, rows)),
             pltpu.SemaphoreType.DMA((5,)),
-            pltpu.SemaphoreType.DMA((4, n)),
-            pltpu.SemaphoreType.DMA((4, n)),
-            pltpu.SemaphoreType.DMA((2, n)),
-            pltpu.SemaphoreType.DMA((2, n)),
+            pltpu.SemaphoreType.DMA((6,)),
+            pltpu.SemaphoreType.DMA((6,)),
         ],
         compiler_params=pltpu.CompilerParams(
             collective_id=0, has_side_effects=True, vmem_limit_bytes=60 * 2**20
@@ -651,13 +633,14 @@
         key_cache,
         value_cache,
         lengths,
-        attention_ids,
-        attention_ids,
-        expert_ids,
-        attention_router,
-        expert_router,
+        attention_ids.T,
+        attention_ids.T,
+        expert_ids.T,
+        attention_router.T,
+        expert_router.T,
         attention_output,
-        gains,
+        expert_gain.reshape(n, LANES),
+        final_gain.reshape(n, LANES),
         expert_gate,
         expert_up,
         expert_down,

time: 65.8 us -> 57.9 us (0.88)
  local copies, waits for them, and re-layouts: 9.1 us -> 1.47 us
  Pallas kernels: 55.6 us -> 56.3 us
    unnamed x5 -> x1, local copies, waits for them, and re-layouts: 7.72 us -> 1.47 us
    another operation x2 -> x0, local copies, waits for them, and re-layouts: 1.39 us -> none  [fused(): gains = jnp.stack([expert_gain, final_gain]).astype(F32)]
where the time goes in v2:
time: 57.9 us; the launch traced here: 57.7 us
  Pallas kernels  56.3 us (97%)
  local copies, waits for them, and re-layouts  1.47 us (3%)
    pallas_call x1, Pallas kernels, fused(): pl.pallas_call(lambda *refs: step_kernel(n_blk, n_req, *refs), out_shape=...  56.3 us
    unnamed x1, local copies, waits for them, and re-layouts  1.47 us

profile of v2, /device:TPU:0, one launch (start us, length us, event | category | flops | bytes accessed | tf_op | source)
XLA Modules:
  0.0 57.7 jit_solution(18118612552404926802)
XLA Ops:
  0.0 56.3 %shard_map.181 = f32[8,2000]{1,0:T(8,128)} custom-call(bf16[1,16,2048]{2,1,0:T(8,128)(2,1)} %refs_0_.1, bf16[1,4,4096]{2,1,0:T(4,128)(2,1)} %refs_1_.1, bf16[1,4,2,2048]{3,2,1,0:T(2,128)(2,1)} %refs_2_.1, bf16[1,4,48,2048]{3,2,1,0:T(8,128)(2,1)} %refs_3_.1, bf16[1,4,48,2048]{3,2,1,0:T(8,128)(2,1)} %refs_4_.1, s32[1,4]{1,0:T(1,128)} %refs_5_.1, ...), custom_call_target="tpu_custom_call" | custom-call | flops 751828992 | bytes 46989312 | tf_op jit(solution)/shard_map/pallas_call | solution.py:590
  56.3 1.5 %copy.21 = f32[8,2000]{1,0:T(8,128)} copy(f32[8,2000]{1,0:T(8,128)} %shard_map.181) | data formatting | bytes 128000

commit v3 on v2

--- a/solution.py
+++ b/solution.py
@@ -214,6 +214,14 @@
         jnp.int32, (extent, extent), 1
     )
     return jnp.sum(jnp.where(diagonal, row, 0.0), axis=1, keepdims=True)
+
+
+def as_row(column):
+    extent = column.shape[0]
+    diagonal = lax.broadcasted_iota(jnp.int32, (extent, extent), 0) == lax.broadcasted_iota(
+        jnp.int32, (extent, extent), 1
+    )
+    return jnp.sum(jnp.where(diagonal, column, 0.0), axis=0, keepdims=True)
 
 
 def step_kernel(
@@ -263,6 +271,9 @@
     w_sem,
     sems_s,
     sems_r,
+    sems_g,
+    sems_f,
+    gain_rows,
 ):
     n = n_blk * n_req
     cfg = lax.axis_index("cfg")
@@ -305,9 +316,55 @@
         (w_down, v_down),
         (w_head, v_head),
     ):
-        copy = pltpu.make_async_copy(source, target, w_sem.at[len(weight_copies)])
-        copy.start()
-        weight_copies.append(copy)
+        extent = source.shape[0]
+        sem = w_sem.at[len(weight_copies)]
+        for first in range(0, extent, 512):
+            cut = pl.ds(first, min(512, extent - first))
+            pltpu.make_async_copy(source.at[cut], target.at[cut], sem).start()
+        weight_copies.append(pltpu.make_async_copy(source, target, sem))
+
+    upper = blk // 2
+    near = (blk, 4 * upper + 1 - blk, 2 - upper, 3 - 3 * upper)
+    columns = n_req * LANES
+
+    def send_plane(source_of, target, plane, own, side, send_sem, recv_sem):
+        def go(k, carry):
+            to = lax.rem(req + k, n_req)
+            pltpu.make_async_remote_copy(
+                src_ref=source_of(plane * n_req + to),
+                dst_ref=target.at[me],
+                send_sem=send_sem,
+                recv_sem=recv_sem,
+                device_id=(side, plane, to),
+                device_id_type=MESH,
+            ).start()
+            return carry
+
+        lax.fori_loop(1 if own else 0, n_req, go, 0, unroll=True)
+
+    def wait_plane(target, count, sem):
+        blocks = target.at[pl.ds(0, count)]
+        pltpu.make_async_remote_copy(
+            src_ref=blocks,
+            dst_ref=blocks,
+            send_sem=sem,
+            recv_sem=sem,
+            device_id=(1 - cfg, blk, req),
+            device_id_type=MESH,
+        ).wait_recv()
+
+    def plane_of(buf, plane):
+        return jnp.concatenate(
+            [buf[plane * n_req + j].astype(F32) for j in range(n_req)], axis=1
+        )
+
+    def gain_of(buf, plane):
+        return jnp.concatenate(
+            [buf[pl.ds(plane * n_req + j, 1), :] for j in range(n_req)], axis=1
+        )
+
+    def columns_of(plane):
+        return pl.ds(pl.multiple_of(plane * columns, columns), columns)
 
     def start_all(source_of, target, phase):
         def go(k, carry):
@@ -398,15 +455,41 @@
             send_a[2 * e + side] = jnp.concatenate([block, stats], axis=0).astype(BF16)
 
     pl.semaphore_wait(barrier, 2 * n - 1)
-    start_all(lambda other: send_a.at[other], recv_a, 0)
+
+    @pl.when(cfg * blk == 0)
+    def _():
+        start_all(lambda other: send_a.at[other], recv_a, 0)
+
+    @pl.when(cfg == 1)
+    def _():
+        spot = (n - n_req, 3 * H, LANES)
+        row = lax.broadcasted_iota(jnp.int32, spot, 1)
+        column = lax.broadcasted_iota(jnp.int32, spot, 2)
+        empty = (row >= 2 * H) & ((column == 0) | (column == 3))
+        recv_a[pl.ds(n_req, n - n_req)] = jnp.where(empty, DEAD, 0.0).astype(BF16)
+
     recv_a[me] = send_a[me]
+    gain_rows[0] = gain_in[...].astype(F32)
+    gain_rows[1] = gain_out[...].astype(F32)
 
     inputs = residual[0].astype(F32)
     normed = rms_scale(inputs).astype(BF16)
     att_logits = dot_nt(att_router[...], normed)
     att_share = as_column(expert_share_of(att_logits, att_ids[...], me // 2))
     weight_copies[0].wait()
-    all_blocks(recv_a, 0).wait_recv()
+
+    @pl.when(cfg == 0)
+    def _():
+        wait_plane(recv_a, n - 1, sems_r.at[0])
+
+    @pl.when(cfg * (blk + 1) == 1)
+    def _():
+        wait_plane(recv_a, n_req - 1, sems_r.at[0])
+
+    @pl.when(cfg * blk > 0)
+    def _():
+        wait_plane(recv_a, n_req, sems_r.at[0])
+
 
     small = lax.broadcasted_iota(jnp.int32, (H, LANES), 1)
     for q in range(n_req):
@@ -436,11 +519,23 @@
     )
     selected = (gathered * att_share).astype(BF16)
 
-    def scatter(product_of, send_buf):
-        for t in range(4):
-            part = product_of(t)
-            for j in range(4):
-                send_buf[4 * t + j] = part[:, j * LANES : (j + 1) * LANES].astype(BF16)
+    def scatter(left, weights, send_buf, target, phase):
+        for step in range(n_blk):
+            plane = near[n_blk - 1 - step]
+            part = jnp.dot(left, weights[:, columns_of(plane)], preferred_element_type=F32)
+            for j in range(n_req):
+                send_buf[plane * n_req + j] = part[:, j * LANES : (j + 1) * LANES].astype(BF16)
+            send_plane(
+                lambda other: send_buf.at[other],
+                target,
+                plane,
+                step == n_blk - 1,
+                cfg,
+                sems_s.at[phase],
+                sems_r.at[phase],
+            )
+        target[me] = send_buf[me]
+        all_blocks(target, phase).wait_recv()
 
     def summed(buf):
         total = buf[0].astype(F32)
@@ -448,95 +543,60 @@
             total = total + buf[k].astype(F32)
         return total
 
-    def whole(buf):
-        return jnp.concatenate([buf[k].astype(F32) for k in range(n)], axis=1)
-
-    def gain_row(gain):
-        wide = gain[...].astype(F32)
-        return jnp.concatenate([wide[k : k + 1] for k in range(n)], axis=1)
-
-    scatter(
-        lambda t: jnp.dot(
-            selected, v_proj[:, t * 512 : (t + 1) * 512], preferred_element_type=F32
-        ),
-        send_r,
-    )
-    start_all(lambda other: send_r.at[other], recv_r, 1)
-    recv_r[me] = send_r[me]
-    all_blocks(recv_r, 1).wait_recv()
+    def squares(values):
+        return jnp.sum(values * values, axis=1, keepdims=True)
+
+    scatter(selected, v_proj, send_r, recv_r, 1)
     own_column = pl.multiple_of(me * LANES, LANES)
     own_middle[...] = summed(recv_r) + residual[0, :, pl.ds(own_column, LANES)].astype(F32)
     send_g[...] = own_middle[...].astype(BF16)
-    start_all(lambda other: send_g, recv_g, 2)
+    for step in range(n_blk):
+        plane = near[n_blk - 1 - step]
+        send_plane(
+            lambda other: send_g, recv_g, plane, step == n_blk - 1, cfg, sems_s.at[2], sems_g.at[blk]
+        )
     recv_g[me] = send_g[...]
     weight_copies[1].wait()
     weight_copies[2].wait()
-    all_blocks(recv_g, 2).wait_recv()
-
-    expert_input = (rms_scale(whole(recv_g)) * gain_row(gain_in)).astype(BF16)
-    share = expert_share_of(
-        dot_nt(exp_router[...], expert_input), exp_ids[...], me * v_gate.shape[0] // FF
-    )
-    tile = v_gate.shape[0] // 2
-    pieces = []
-    for t in range(2):
-        gate_values = dot_nt(v_gate[t * tile : (t + 1) * tile, :], expert_input)
-        up_values = dot_nt(v_up[t * tile : (t + 1) * tile, :], expert_input)
-        part = jax.nn.silu(gate_values) * up_values * share
-        pieces.append(jnp.transpose(part).astype(BF16))
+    square_sum = 0.0
+    gate_sum = 0.0
+    up_sum = 0.0
+    router_sum = 0.0
+    for step in range(n_blk):
+        plane = near[step]
+        wait_plane(recv_g, n_req - 1 if step == 0 else n_req, sems_g.at[plane])
+        part = plane_of(recv_g, plane)
+        square_sum = square_sum + squares(part)
+        part = (part * gain_of(gain_rows.at[0], plane)).astype(BF16)
+        gate_sum = gate_sum + dot_nt(part, v_gate[:, columns_of(plane)])
+        up_sum = up_sum + dot_nt(part, v_up[:, columns_of(plane)])
+        router_sum = router_sum + dot_nt(exp_router[:, columns_of(plane)], part)
+    scale = lax.rsqrt(square_sum / (n * LANES) + EPS)
+    share = as_column(
+        expert_share_of(
+            router_sum * as_row(scale), exp_ids[...], me * v_gate.shape[0] // FF
+        )
+    )
+    all_hidden = (jax.nn.silu(gate_sum * scale) * (up_sum * (scale * share))).astype(BF16)
     weight_copies[3].wait()
-    all_hidden = jnp.concatenate(pieces, axis=1)
-    scatter(
-        lambda t: jnp.dot(
-            all_hidden, v_down[:, t * 512 : (t + 1) * 512], preferred_element_type=F32
-        ),
-        send_q,
-    )
-    start_all(lambda other: send_q.at[other], recv_q, 3)
-    recv_q[me] = send_q[me]
-    all_blocks(recv_q, 3).wait_recv()
+    scatter(all_hidden, v_down, send_q, recv_q, 3)
     send_f[...] = (own_middle[...] + summed(recv_q)).astype(BF16)
-
-    def final_send(away, other):
-        side = 1 - cfg if away else cfg
-        pltpu.make_async_remote_copy(
-            src_ref=send_f,
-            dst_ref=recv_f.at[cfg, me],
-            send_sem=sems_s.at[4 + away],
-            recv_sem=sems_r.at[4 + away],
-            device_id=(side, other // n_req, lax.rem(other, n_req)),
-            device_id_type=MESH,
-        ).start()
-
-    def final_step(k, carry):
-        other = lax.rem(me + k, n)
-        final_send(0, other)
-        final_send(1, other)
-        return carry
-
-    lax.fori_loop(1, n, final_step, 0, unroll=True)
-    final_send(1, me)
+    for step in range(n_blk):
+        plane = near[n_blk - 1 - step]
+        for away in (0, 1):
+            send_plane(
+                lambda other: send_f,
+                recv_f.at[cfg],
+                plane,
+                step == n_blk - 1 and away == 0,
+                1 - cfg if away else cfg,
+                sems_s.at[4 + away],
+                sems_f.at[away, blk],
+            )
     recv_f[cfg, me] = send_f[...]
     weight_copies[4].wait()
-    for away in (0, 1):
-        target = recv_f.at[0, pl.ds(0, n - 1 + away)]
-        pltpu.make_async_remote_copy(
-            src_ref=target,
-            dst_ref=target,
-            send_sem=sems_s.at[4 + away],
-            recv_sem=sems_r.at[4 + away],
-            device_id=(1 - cfg, blk, req),
-            device_id_type=MESH,
-        ).wait()
-    for phase, target in enumerate((recv_a, recv_r, recv_g, recv_q)):
-        all_blocks(target, phase).wait_send()
 
     guided_rows = out.shape[0]
-    mine = []
-    for stream in (0, 1):
-        both = whole(recv_f.at[stream])
-        mine.append(jnp.where(cfg == 0, both[:guided_rows], both[guided_rows:]))
-    final_input = (rms_scale(jnp.concatenate(mine, axis=0)) * gain_row(gain_out)).astype(BF16)
     request = cfg * guided_rows + lax.broadcasted_iota(jnp.int32, (guided_rows, LANES), 0)
     tenant = jnp.zeros_like(request)
     end = 0
@@ -547,12 +607,42 @@
     for t in range(sizes.shape[0]):
         guide = guide + jnp.where(tenant == t, guidance[t], 0)
     factor = guide.astype(F32)[:, 0:1] / 4.0
-    words = v_head.shape[0]
-    for first in range(0, words, 1024):
-        last = min(first + 1024, words)
-        logits = jnp.transpose(dot_nt(v_head[first:last, :], final_input))
-        conditional, unconditional = logits[:guided_rows], logits[guided_rows:]
-        out[:, first:last] = unconditional + factor * (conditional - unconditional)
+    square_sum = 0.0
+    logits = 0.0
+    for step in range(n_blk):
+        plane = near[step]
+        for away in (0, 1):
+            wait_plane(
+                recv_f.at[0],
+                n_req - 1 if step == 0 and away == 0 else n_req,
+                sems_f.at[away, plane],
+            )
+        mine = []
+        for stream in (0, 1):
+            both = plane_of(recv_f.at[stream], plane)
+            mine.append(jnp.where(cfg == 0, both[:guided_rows], both[guided_rows:]))
+        part = jnp.concatenate(mine, axis=0)
+        square_sum = square_sum + squares(part)
+        part = (part * gain_of(gain_rows.at[1], plane)).astype(BF16)
+        logits = logits + dot_nt(part, v_head[:, columns_of(plane)])
+    logits = logits * lax.rsqrt(square_sum / (n * LANES) + EPS)
+    conditional, unconditional = logits[:guided_rows], logits[guided_rows:]
+    out[...] = unconditional + factor * (conditional - unconditional)
+
+    @pl.when(cfg * blk == 0)
+    def _():
+        all_blocks(recv_a, 0).wait_send()
+
+    for phase, target in ((1, recv_r), (2, recv_g), (3, recv_q), (4, recv_f.at[0])):
+        all_blocks(target, phase).wait_send()
+    pltpu.make_async_remote_copy(
+        src_ref=recv_f.at[0],
+        dst_ref=recv_f.at[0],
+        send_sem=sems_s.at[5],
+        recv_sem=sems_r.at[0],
+        device_id=(1 - cfg, blk, req),
+        device_id_type=MESH,
+    ).wait_send()
 
 
 def fused(
@@ -618,7 +708,10 @@
             pltpu.SemaphoreType.DMA((2, rows)),
             pltpu.SemaphoreType.DMA((5,)),
             pltpu.SemaphoreType.DMA((6,)),
-            pltpu.SemaphoreType.DMA((6,)),
+            pltpu.SemaphoreType.DMA((4,)),
+            pltpu.SemaphoreType.DMA((n_blk,)),
+            pltpu.SemaphoreType.DMA((2, n_blk)),
+            pltpu.VMEM((2, n, LANES), F32),
         ],
         compiler_params=pltpu.CompilerParams(
             collective_id=0, has_side_effects=True, vmem_limit_bytes=60 * 2**20

time: 57.9 us -> 56.4 us (0.974)
  Pallas kernels: 56.3 us -> 54.8 us
    pallas_call x1, Pallas kernels: 56.3 us -> 54.8 us  [fused(): pl.pallas_call(lambda *refs: step_kernel(n_blk, n_req, *refs), out_shape=...]
where the time goes in v3:
time: 56.4 us; the launch traced here: 56.2 us
  Pallas kernels  54.8 us (97%)
  local copies, waits for them, and re-layouts  1.47 us (3%)
    pallas_call x1, Pallas kernels, fused(): pl.pallas_call(lambda *refs: step_kernel(n_blk, n_req, *refs), out_shape=...  54.8 us
    unnamed x1, local copies, waits for them, and re-layouts  1.47 us

profile of v3, /device:TPU:0, one launch (start us, length us, event | category | flops | bytes accessed | tf_op | source)
XLA Modules:
  0.0 56.2 jit_solution(8907804446642380890)
XLA Ops:
  0.0 54.8 %shard_map.181 = f32[8,2000]{1,0:T(8,128)} custom-call(bf16[1,16,2048]{2,1,0:T(8,128)(2,1)} %refs_0_.1, bf16[1,4,4096]{2,1,0:T(4,128)(2,1)} %refs_1_.1, bf16[1,4,2,2048]{3,2,1,0:T(2,128)(2,1)} %refs_2_.1, bf16[1,4,48,2048]{3,2,1,0:T(8,128)(2,1)} %refs_3_.1, bf16[1,4,48,2048]{3,2,1,0:T(8,128)(2,1)} %refs_4_.1, s32[1,4]{1,0:T(1,128)} %refs_5_.1, ...), custom_call_target="tpu_custom_call" | custom-call | flops 751828992 | bytes 46989312 | tf_op jit(solution)/shard_map/pallas_call | solution.py:680
  54.8 1.5 %copy.21 = f32[8,2000]{1,0:T(8,128)} copy(f32[8,2000]{1,0:T(8,128)} %shard_map.181) | data formatting | bytes 128000

commit v4 on v3

--- a/solution.py
+++ b/solution.py
@@ -199,13 +199,16 @@
     return lax.dot_general(left, right, (((1,), (1,)), ((), ())), preferred_element_type=F32)
 
 
-def expert_share_of(logits, ids, expert):
+def gates_of(logits, ids):
     experts = lax.broadcasted_iota(jnp.int32, logits.shape, 0)
     first = jnp.sum(jnp.where(experts == ids[0:1], logits, 0.0), axis=0, keepdims=True)
     second = jnp.sum(jnp.where(experts == ids[1:2], logits, 0.0), axis=0, keepdims=True)
-    return jnp.where(ids[0:1] == expert, jax.nn.sigmoid(first - second), 0.0) + jnp.where(
-        ids[1:2] == expert, jax.nn.sigmoid(second - first), 0.0
-    )
+    return jax.nn.sigmoid(first - second), jax.nn.sigmoid(second - first)
+
+
+def expert_share_of(logits, ids, expert):
+    first, second = gates_of(logits, ids)
+    return jnp.where(ids[0:1] == expert, first, 0.0) + jnp.where(ids[1:2] == expert, second, 0.0)
 
 
 def as_column(row):
@@ -234,7 +237,6 @@
     value_cache,
     lengths,
     att_ids,
-    att_ids_s,
     exp_ids,
     att_router,
     exp_router,
@@ -271,9 +273,12 @@
     w_sem,
     sems_s,
     sems_r,
+    sems_a,
     sems_g,
-    sems_f,
     gain_rows,
+    send_l,
+    recv_l,
+    swap_sem,
 ):
     n = n_blk * n_req
     cfg = lax.axis_index("cfg")
@@ -316,34 +321,44 @@
         (w_down, v_down),
         (w_head, v_head),
     ):
-        extent = source.shape[0]
+        extent = target.shape[0]
+        own_first = cfg * (source.shape[0] - extent)
         sem = w_sem.at[len(weight_copies)]
         for first in range(0, extent, 512):
-            cut = pl.ds(first, min(512, extent - first))
-            pltpu.make_async_copy(source.at[cut], target.at[cut], sem).start()
-        weight_copies.append(pltpu.make_async_copy(source, target, sem))
+            size = min(512, extent - first)
+            pltpu.make_async_copy(
+                source.at[pl.ds(pl.multiple_of(own_first + first, 16), size)],
+                target.at[pl.ds(first, size)],
+                sem,
+            ).start()
+        weight_copies.append(
+            pltpu.make_async_copy(source.at[pl.ds(0, extent)], target, sem)
+        )
 
     upper = blk // 2
     near = (blk, 4 * upper + 1 - blk, 2 - upper, 3 - 3 * upper)
     columns = n_req * LANES
 
-    def send_plane(source_of, target, plane, own, side, send_sem, recv_sem):
-        def go(k, carry):
-            to = lax.rem(req + k, n_req)
-            pltpu.make_async_remote_copy(
-                src_ref=source_of(plane * n_req + to),
-                dst_ref=target.at[me],
-                send_sem=send_sem,
-                recv_sem=recv_sem,
-                device_id=(side, plane, to),
-                device_id_type=MESH,
-            ).start()
-            return carry
-
-        lax.fori_loop(1 if own else 0, n_req, go, 0, unroll=True)
+    def send_plane(source_of, target, plane, own, phase, recv_sem_of):
+        for away in (0, 1):
+            side = 1 - cfg if away else cfg
+
+            def go(k, carry, away=away, side=side):
+                to = lax.rem(req + k, n_req)
+                pltpu.make_async_remote_copy(
+                    src_ref=source_of(side, plane * n_req + to),
+                    dst_ref=target.at[cfg, me],
+                    send_sem=sems_s.at[phase, away],
+                    recv_sem=recv_sem_of(away),
+                    device_id=(side, plane, to),
+                    device_id_type=MESH,
+                ).start()
+                return carry
+
+            lax.fori_loop(1 if own and away == 0 else 0, n_req, go, 0, unroll=True)
 
     def wait_plane(target, count, sem):
-        blocks = target.at[pl.ds(0, count)]
+        blocks = target.at[0, pl.ds(0, count)]
         pltpu.make_async_remote_copy(
             src_ref=blocks,
             dst_ref=blocks,
@@ -353,9 +368,27 @@
             device_id_type=MESH,
         ).wait_recv()
 
+    def wait_sent(target, phase):
+        for away in (0, 1):
+            blocks = target.at[0, pl.ds(0, n - 1 + away)]
+            pltpu.make_async_remote_copy(
+                src_ref=blocks,
+                dst_ref=blocks,
+                send_sem=sems_s.at[phase, away],
+                recv_sem=sems_s.at[phase, away],
+                device_id=(1 - cfg, blk, req),
+                device_id_type=MESH,
+            ).wait_send()
+
     def plane_of(buf, plane):
         return jnp.concatenate(
-            [buf[plane * n_req + j].astype(F32) for j in range(n_req)], axis=1
+            [
+                jnp.concatenate(
+                    [buf[stream, plane * n_req + j].astype(F32) for j in range(n_req)], axis=1
+                )
+                for stream in (0, 1)
+            ],
+            axis=0,
         )
 
     def gain_of(buf, plane):
@@ -365,31 +398,6 @@
 
     def columns_of(plane):
         return pl.ds(pl.multiple_of(plane * columns, columns), columns)
-
-    def start_all(source_of, target, phase):
-        def go(k, carry):
-            other = lax.rem(me + k, n)
-            pltpu.make_async_remote_copy(
-                src_ref=source_of(other),
-                dst_ref=target.at[me],
-                send_sem=sems_s.at[phase],
-                recv_sem=sems_r.at[phase],
-                device_id=(cfg, other // n_req, lax.rem(other, n_req)),
-                device_id_type=MESH,
-            ).start()
-            return carry
-
-        lax.fori_loop(1, n, go, 0, unroll=True)
-
-    def all_blocks(target, phase):
-        return pltpu.make_async_remote_copy(
-            src_ref=target.at[pl.ds(0, n - 1)],
-            dst_ref=target.at[pl.ds(0, n - 1)],
-            send_sem=sems_s.at[phase],
-            recv_sem=sems_r.at[phase],
-            device_id=(1 - cfg, blk, req),
-            device_id_type=MESH,
-        )
 
     extra = keys.shape[1] - local_pos
     head_of_row = lax.rem(lax.broadcasted_iota(jnp.int32, (TOPK * H, 1), 0), H)
@@ -398,6 +406,21 @@
     place = lax.broadcasted_iota(jnp.int32, (1, keys.shape[1]), 1)
     new_row = lax.broadcasted_iota(jnp.int32, (extra, 1), 0) == 0
     query_all = queries[0].astype(F32)
+    inputs = residual[0].astype(F32)
+    normed = rms_scale(inputs).astype(BF16)
+    ids_here = att_ids[...]
+    chosen = (H, ids_here.shape[1])
+    mine = lax.broadcasted_iota(jnp.int32, chosen, 1) == (
+        req * rows + lax.broadcasted_iota(jnp.int32, chosen, 0) // (H // rows)
+    )
+    gate_columns = [
+        jnp.sum(jnp.where(mine, gate, 0.0), axis=1, keepdims=True)
+        for gate in gates_of(dot_nt(att_router[...], normed), ids_here)
+    ]
+    id_columns = [
+        jnp.sum(jnp.where(mine, ids_here[k : k + 1], 0), axis=1, keepdims=True)
+        for k in range(TOPK)
+    ]
     outs = []
     tops = []
     for copy in cache_copies:
@@ -429,119 +452,139 @@
         outs.append(acc / safe)
         tops.append(jnp.where(alive, top + jnp.log(safe), DEAD))
 
-    lane = lax.broadcasted_iota(jnp.int32, (2 * H, LANES), 1)
-    half = H // 2
-    for e in range(n // 2):
-        picked = []
-        levels = []
-        for r in range(rows):
-            first = jnp.where(att_ids_s[0, req * rows + r] == e, 1.0, 0.0)
-            second = jnp.where(att_ids_s[1, req * rows + r] == e, 1.0, 0.0)
-            picked.append(first * outs[r][:H] + second * outs[r][H:])
-            levels.append(first * tops[r][:H] + second * tops[r][H:])
-        for side in range(2):
-            cut = slice(side * half, (side + 1) * half)
-            block = jnp.concatenate([part[cut] for part in picked], axis=0)
-            level = jnp.concatenate([part[cut] for part in levels], axis=0)
+    quarter = H // 4
+    lane = lax.broadcasted_iota(jnp.int32, (H, LANES), 1)
+    for part in range(4):
+        cuts = [slice(k * H + part * quarter, k * H + (part + 1) * quarter) for k in range(TOPK)]
+        blocks = [jnp.concatenate([each[cut] for each in outs], axis=0) for cut in cuts]
+        levels = [jnp.concatenate([each[cut] for each in tops], axis=0) for cut in cuts]
+        for e in range(n // 2):
+            first = id_columns[0] == e
+            second = id_columns[1] == e
+            block = jnp.where(first, gate_columns[0] * blocks[0], 0.0) + jnp.where(
+                second, gate_columns[1] * blocks[1], 0.0
+            )
+            level = jnp.where(first, levels[0], jnp.where(second, levels[1], 0.0))
             high = level.astype(BF16).astype(F32)
             mid = (level - high).astype(BF16).astype(F32)
-            low = level - high - mid
-            parts = jnp.where(
-                lax.rem(lane, 3) == 0, high, jnp.where(lax.rem(lane, 3) == 1, mid, low)
+            stats = jnp.where(
+                lane == 0,
+                high,
+                jnp.where(lane == 1, mid, jnp.where(lane == 2, level - high - mid, 0.0)),
             )
-            stats = jnp.where(
-                lane[:H] < 3, parts[:H], jnp.where(lane[:H] < 6, parts[H:], 0.0)
-            )
-            send_a[2 * e + side] = jnp.concatenate([block, stats], axis=0).astype(BF16)
-
+            send_a[part % 2, 2 * e + part // 2] = jnp.concatenate(
+                [block, stats], axis=0
+            ).astype(BF16)
+
+    spot = (n - n_req, 2 * H, LANES)
+    empty = (lax.broadcasted_iota(jnp.int32, spot, 1) >= H) & (
+        lax.broadcasted_iota(jnp.int32, spot, 2) == 0
+    )
+    recv_a[1, pl.ds(n_req, n - n_req)] = jnp.where(empty, DEAD, 0.0).astype(BF16)
     pl.semaphore_wait(barrier, 2 * n - 1)
 
     @pl.when(cfg * blk == 0)
     def _():
-        start_all(lambda other: send_a.at[other], recv_a, 0)
+        for step in range(n_blk):
+            send_plane(
+                lambda side, other: send_a.at[side, other],
+                recv_a,
+                near[n_blk - 1 - step],
+                step == n_blk - 1,
+                0,
+                lambda away: sems_a.at[cfg],
+            )
+
+    recv_a[cfg, me] = send_a[cfg, me]
+    gain_rows[0] = gain_in[...].astype(F32)
+    gain_rows[1] = gain_out[...].astype(F32)
+    weight_copies[0].wait()
+
+    @pl.when(cfg == 0)
+    def _():
+        wait_plane(recv_a, n - 1, sems_a.at[0])
+        wait_plane(recv_a, n_req, sems_a.at[1])
 
     @pl.when(cfg == 1)
     def _():
-        spot = (n - n_req, 3 * H, LANES)
-        row = lax.broadcasted_iota(jnp.int32, spot, 1)
-        column = lax.broadcasted_iota(jnp.int32, spot, 2)
-        empty = (row >= 2 * H) & ((column == 0) | (column == 3))
-        recv_a[pl.ds(n_req, n - n_req)] = jnp.where(empty, DEAD, 0.0).astype(BF16)
-
-    recv_a[me] = send_a[me]
-    gain_rows[0] = gain_in[...].astype(F32)
-    gain_rows[1] = gain_out[...].astype(F32)
-
-    inputs = residual[0].astype(F32)
-    normed = rms_scale(inputs).astype(BF16)
-    att_logits = dot_nt(att_router[...], normed)
-    att_share = as_column(expert_share_of(att_logits, att_ids[...], me // 2))
-    weight_copies[0].wait()
-
-    @pl.when(cfg == 0)
-    def _():
-        wait_plane(recv_a, n - 1, sems_r.at[0])
+        wait_plane(recv_a, n, sems_a.at[0])
 
     @pl.when(cfg * (blk + 1) == 1)
     def _():
-        wait_plane(recv_a, n_req - 1, sems_r.at[0])
+        wait_plane(recv_a, n_req - 1, sems_a.at[1])
 
     @pl.when(cfg * blk > 0)
     def _():
-        wait_plane(recv_a, n_req, sems_r.at[0])
-
-
-    small = lax.broadcasted_iota(jnp.int32, (H, LANES), 1)
-    for q in range(n_req):
-        blocks = []
-        levels = []
-        for b in range(n_blk):
-            message = recv_a[b * n_req + q].astype(F32)
-            stats = message[2 * H :]
-            upper = jnp.sum(jnp.where(small < 3, stats, 0.0), axis=1, keepdims=True)
-            lower = jnp.sum(
-                jnp.where((small >= 3) & (small < 6), stats, 0.0), axis=1, keepdims=True
-            )
-            levels.append(jnp.concatenate([upper, lower], axis=0))
-            blocks.append(message[: 2 * H])
-        peak = levels[0]
-        for b in range(1, n_blk):
-            peak = jnp.maximum(peak, levels[b])
-        total = jnp.zeros_like(peak)
-        mixed = jnp.zeros_like(blocks[0])
-        for b in range(n_blk):
-            weight = jnp.exp(levels[b] - peak)
-            total = total + weight
-            mixed = mixed + weight * blocks[b]
-        joint[pl.ds(q * 2 * H, 2 * H)] = (mixed / total).astype(BF16).astype(F32)
+        wait_plane(recv_a, n_req, sems_a.at[1])
+
+    for stream in (0, 1):
+        for q in range(n_req):
+            blocks = []
+            levels = []
+            for b in range(n_blk):
+                message = recv_a[stream, b * n_req + q].astype(F32)
+                levels.append(jnp.sum(message[H:], axis=1, keepdims=True))
+                blocks.append(message[:H])
+            peak = levels[0]
+            for b in range(1, n_blk):
+                peak = jnp.maximum(peak, levels[b])
+            total = jnp.zeros_like(peak)
+            mixed = jnp.zeros_like(blocks[0])
+            for b in range(n_blk):
+                weight = jnp.exp(levels[b] - peak)
+                total = total + weight
+                mixed = mixed + weight * blocks[b]
+            joint[pl.ds((stream * n_req + q) * H, H)] = mixed / total
     gathered = jnp.concatenate(
-        [joint[pl.ds(h, n_req * rows, stride=half), :] for h in range(half)], axis=1
-    )
-    selected = (gathered * att_share).astype(BF16)
+        [joint[pl.ds(h, 2 * n_req * rows, stride=quarter), :] for h in range(quarter)], axis=1
+    )
+    selected = gathered.astype(BF16)
 
     def scatter(left, weights, send_buf, target, phase):
         for step in range(n_blk):
             plane = near[n_blk - 1 - step]
             part = jnp.dot(left, weights[:, columns_of(plane)], preferred_element_type=F32)
-            for j in range(n_req):
-                send_buf[plane * n_req + j] = part[:, j * LANES : (j + 1) * LANES].astype(BF16)
+            for stream in (0, 1):
+                for j in range(n_req):
+                    send_buf[stream, plane * n_req + j] = part[
+                        stream * H : (stream + 1) * H, j * LANES : (j + 1) * LANES
+                    ].astype(BF16)
             send_plane(
-                lambda other: send_buf.at[other],
+                lambda side, other: send_buf.at[side, other],
                 target,
                 plane,
                 step == n_blk - 1,
-                cfg,
-                sems_s.at[phase],
-                sems_r.at[phase],
+                phase,
+                lambda away: sems_r.at[phase, away],
             )
-        target[me] = send_buf[me]
-        all_blocks(target, phase).wait_recv()
+        target[cfg, me] = send_buf[cfg, me]
+        wait_plane(target, n - 1, sems_r.at[phase, 0])
+        wait_plane(target, n, sems_r.at[phase, 1])
 
     def summed(buf):
-        total = buf[0].astype(F32)
-        for k in range(1, n):
-            total = total + buf[k].astype(F32)
+        total = 0.0
+        for stream in (0, 1):
+            for k in range(n):
+                total = total + buf[stream, k].astype(F32)
         return total
+
+    def gather(block, target, phase):
+        for step in range(n_blk):
+            send_plane(
+                lambda side, other: block,
+                target,
+                near[n_blk - 1 - step],
+                step == n_blk - 1,
+                phase,
+                lambda away: sems_g.at[phase, away, blk],
+            )
+        target[cfg, me] = block[...]
+
+    def gathered_plane(step, target, phase):
+        plane = near[step]
+        wait_plane(target, n_req - 1 if step == 0 else n_req, sems_g.at[phase, 0, plane])
+        wait_plane(target, n_req, sems_g.at[phase, 1, plane])
+        return plane, plane_of(target, plane)
 
     def squares(values):
         return jnp.sum(values * values, axis=1, keepdims=True)
@@ -550,12 +593,7 @@
     own_column = pl.multiple_of(me * LANES, LANES)
     own_middle[...] = summed(recv_r) + residual[0, :, pl.ds(own_column, LANES)].astype(F32)
     send_g[...] = own_middle[...].astype(BF16)
-    for step in range(n_blk):
-        plane = near[n_blk - 1 - step]
-        send_plane(
-            lambda other: send_g, recv_g, plane, step == n_blk - 1, cfg, sems_s.at[2], sems_g.at[blk]
-        )
-    recv_g[me] = send_g[...]
+    gather(send_g, recv_g, 2)
     weight_copies[1].wait()
     weight_copies[2].wait()
     square_sum = 0.0
@@ -563,9 +601,7 @@
     up_sum = 0.0
     router_sum = 0.0
     for step in range(n_blk):
-        plane = near[step]
-        wait_plane(recv_g, n_req - 1 if step == 0 else n_req, sems_g.at[plane])
-        part = plane_of(recv_g, plane)
+        plane, part = gathered_plane(step, recv_g, 2)
         square_sum = square_sum + squares(part)
         part = (part * gain_of(gain_rows.at[0], plane)).astype(BF16)
         gate_sum = gate_sum + dot_nt(part, v_gate[:, columns_of(plane)])
@@ -574,30 +610,20 @@
     scale = lax.rsqrt(square_sum / (n * LANES) + EPS)
     share = as_column(
         expert_share_of(
-            router_sum * as_row(scale), exp_ids[...], me * v_gate.shape[0] // FF
+            router_sum * as_row(scale),
+            jnp.concatenate([exp_ids[...]] * 2, axis=1),
+            2 * me * v_gate.shape[0] // FF,
         )
     )
     all_hidden = (jax.nn.silu(gate_sum * scale) * (up_sum * (scale * share))).astype(BF16)
     weight_copies[3].wait()
     scatter(all_hidden, v_down, send_q, recv_q, 3)
     send_f[...] = (own_middle[...] + summed(recv_q)).astype(BF16)
-    for step in range(n_blk):
-        plane = near[n_blk - 1 - step]
-        for away in (0, 1):
-            send_plane(
-                lambda other: send_f,
-                recv_f.at[cfg],
-                plane,
-                step == n_blk - 1 and away == 0,
-                1 - cfg if away else cfg,
-                sems_s.at[4 + away],
-                sems_f.at[away, blk],
-            )
-    recv_f[cfg, me] = send_f[...]
+    gather(send_f, recv_f, 4)
     weight_copies[4].wait()
 
     guided_rows = out.shape[0]
-    request = cfg * guided_rows + lax.broadcasted_iota(jnp.int32, (guided_rows, LANES), 0)
+    request = lax.broadcasted_iota(jnp.int32, (2 * guided_rows, LANES), 0)
     tenant = jnp.zeros_like(request)
     end = 0
     for t in range(sizes.shape[0]):
@@ -610,39 +636,37 @@
     square_sum = 0.0
     logits = 0.0
     for step in range(n_blk):
-        plane = near[step]
-        for away in (0, 1):
-            wait_plane(
-                recv_f.at[0],
-                n_req - 1 if step == 0 and away == 0 else n_req,
-                sems_f.at[away, plane],
-            )
-        mine = []
-        for stream in (0, 1):
-            both = plane_of(recv_f.at[stream], plane)
-            mine.append(jnp.where(cfg == 0, both[:guided_rows], both[guided_rows:]))
-        part = jnp.concatenate(mine, axis=0)
+        plane, part = gathered_plane(step, recv_f, 4)
         square_sum = square_sum + squares(part)
         part = (part * gain_of(gain_rows.at[1], plane)).astype(BF16)
         logits = logits + dot_nt(part, v_head[:, columns_of(plane)])
     logits = logits * lax.rsqrt(square_sum / (n * LANES) + EPS)
-    conditional, unconditional = logits[:guided_rows], logits[guided_rows:]
-    out[...] = unconditional + factor * (conditional - unconditional)
+    conditional, unconditional = logits[:H], logits[H:]
+    guided = unconditional + factor * (conditional - unconditional)
+    lower, upper = guided[:guided_rows], guided[guided_rows:]
+    send_l[...] = jnp.where(cfg == 0, upper, lower)
+    swap = pltpu.make_async_remote_copy(
+        src_ref=send_l,
+        dst_ref=recv_l,
+        send_sem=swap_sem.at[0],
+        recv_sem=swap_sem.at[1],
+        device_id=(1 - cfg, blk, req),
+        device_id_type=MESH,
+    )
+    swap.start()
 
     @pl.when(cfg * blk == 0)
     def _():
-        all_blocks(recv_a, 0).wait_send()
-
-    for phase, target in ((1, recv_r), (2, recv_g), (3, recv_q), (4, recv_f.at[0])):
-        all_blocks(target, phase).wait_send()
-    pltpu.make_async_remote_copy(
-        src_ref=recv_f.at[0],
-        dst_ref=recv_f.at[0],
-        send_sem=sems_s.at[5],
-        recv_sem=sems_r.at[0],
-        device_id=(1 - cfg, blk, req),
-        device_id_type=MESH,
-    ).wait_send()
+        wait_sent(recv_a, 0)
+
+    for phase, target in ((1, recv_r), (2, recv_g), (3, recv_q), (4, recv_f)):
+        wait_sent(target, phase)
+    held = jnp.where(cfg == 0, lower, upper)
+    swap.wait()
+    other_words = recv_l[...]
+    words = v_head.shape[0]
+    out[:, :words] = jnp.where(cfg == 0, held, other_words)
+    out[:, words:] = jnp.where(cfg == 0, other_words, held)[:, 2 * words - out.shape[1] :]
 
 
 def fused(
@@ -672,6 +696,8 @@
     rows = queries.shape[1]
     positions = key_cache.shape[2] + 16
     width = H * HD
+    D = residual.shape[2]
+    head_words = (unembedding.shape[0] // 2 + LANES - 1) // LANES * LANES
     vmem = pl.BlockSpec(memory_space=pltpu.VMEM)
     smem = pl.BlockSpec(memory_space=pltpu.SMEM)
     hbm = pl.BlockSpec(memory_space=pl.ANY)
@@ -681,37 +707,40 @@
         lambda *refs: step_kernel(n_blk, n_req, *refs),
         out_shape=jax.ShapeDtypeStruct((requests // 2, unembedding.shape[0]), F32),
         in_specs=[
-            vmem, vmem, vmem, hbm, hbm, smem, vmem, smem, vmem, vmem, vmem,
+            vmem, vmem, vmem, hbm, hbm, smem, vmem, vmem, vmem, vmem,
             hbm, vmem, vmem, hbm, hbm, hbm, hbm, smem, smem,
         ],
         out_specs=vmem,
         scratch_shapes=[
             pltpu.VMEM((rows, positions, width), BF16),
             pltpu.VMEM((rows, positions, width), BF16),
-            pltpu.VMEM(attention_output.shape, BF16),
-            pltpu.VMEM(expert_gate.shape, BF16),
-            pltpu.VMEM(expert_up.shape, BF16),
-            pltpu.VMEM(expert_down.shape, BF16),
-            pltpu.VMEM(unembedding.shape, BF16),
-            pltpu.VMEM((n, 3 * H, LANES), BF16),
-            pltpu.VMEM((n, 3 * H, LANES), BF16),
-            pltpu.VMEM((requests * H // 2, LANES), F32),
-            pltpu.VMEM((n, *block), BF16),
-            pltpu.VMEM((n, *block), BF16),
+            pltpu.VMEM((attention_output.shape[0] // 2, D), BF16),
+            pltpu.VMEM((expert_gate.shape[0] // 2, D), BF16),
+            pltpu.VMEM((expert_gate.shape[0] // 2, D), BF16),
+            pltpu.VMEM((expert_gate.shape[0] // 2, D), BF16),
+            pltpu.VMEM((head_words, D), BF16),
+            pltpu.VMEM((2, n, 2 * H, LANES), BF16),
+            pltpu.VMEM((2, n, 2 * H, LANES), BF16),
+            pltpu.VMEM((2 * requests * H // 4, LANES), F32),
+            pltpu.VMEM((2, n, *block), BF16),
+            pltpu.VMEM((2, n, *block), BF16),
             pltpu.VMEM(block, BF16),
-            pltpu.VMEM((n, *block), BF16),
-            pltpu.VMEM((n, *block), BF16),
-            pltpu.VMEM((n, *block), BF16),
+            pltpu.VMEM((2, n, *block), BF16),
+            pltpu.VMEM((2, n, *block), BF16),
+            pltpu.VMEM((2, n, *block), BF16),
             pltpu.VMEM(block, BF16),
             pltpu.VMEM((2, n, *block), BF16),
             pltpu.VMEM(block, F32),
             pltpu.SemaphoreType.DMA((2, rows)),
             pltpu.SemaphoreType.DMA((5,)),
-            pltpu.SemaphoreType.DMA((6,)),
-            pltpu.SemaphoreType.DMA((4,)),
-            pltpu.SemaphoreType.DMA((n_blk,)),
-            pltpu.SemaphoreType.DMA((2, n_blk)),
+            pltpu.SemaphoreType.DMA((5, 2)),
+            pltpu.SemaphoreType.DMA((5, 2)),
+            pltpu.SemaphoreType.DMA((2,)),
+            pltpu.SemaphoreType.DMA((5, 2, n_blk)),
             pltpu.VMEM((2, n, LANES), F32),
+            pltpu.VMEM((requests // 2, head_words), F32),
+            pltpu.VMEM((requests // 2, head_words), F32),
+            pltpu.SemaphoreType.DMA((2,)),
         ],
         compiler_params=pltpu.CompilerParams(
             collective_id=0, has_side_effects=True, vmem_limit_bytes=60 * 2**20
@@ -726,7 +755,6 @@
         key_cache,
         value_cache,
         lengths,
-        attention_ids.T,
         attention_ids.T,
         expert_ids.T,
         attention_router.T,

time: 56.4 us -> 49.5 us (0.88)
  Pallas kernels: 54.8 us -> 47.8 us
    pallas_call x1, Pallas kernels: 54.8 us -> 47.8 us  [fused(): pl.pallas_call(lambda *refs: step_kernel(n_blk, n_req, *refs), out_shape=...]
where the time goes in v4:
time: 49.5 us; the launch traced here: 49.3 us
  Pallas kernels  47.8 us (97%)
  local copies, waits for them, and re-layouts  1.47 us (3%)
    pallas_call x1, Pallas kernels, fused(): pl.pallas_call(lambda *refs: step_kernel(n_blk, n_req, *refs), out_shape=...  47.8 us
    unnamed x1, local copies, waits for them, and re-layouts  1.47 us

profile of v4, /device:TPU:0, one launch (start us, length us, event | category | flops | bytes accessed | tf_op | source)
XLA Modules:
  0.0 49.3 jit_solution(10201754610761743079)
XLA Ops:
  0.0 47.8 %shard_map.181 = f32[8,2000]{1,0:T(8,128)} custom-call(bf16[1,16,2048]{2,1,0:T(8,128)(2,1)} %refs_0_.1, bf16[1,4,4096]{2,1,0:T(4,128)(2,1)} %refs_1_.1, bf16[1,4,2,2048]{3,2,1,0:T(2,128)(2,1)} %refs_2_.1, bf16[1,4,48,2048]{3,2,1,0:T(8,128)(2,1)} %refs_3_.1, bf16[1,4,48,2048]{3,2,1,0:T(8,128)(2,1)} %refs_4_.1, s32[1,4]{1,0:T(1,128)} %refs_5_.1, ...), custom_call_target="tpu_custom_call" | custom-call | flops 751828992 | bytes 46989312 | tf_op jit(solution)/shard_map/pallas_call | solution.py:706
  47.9 1.5 %copy.21 = f32[8,2000]{1,0:T(8,128)} copy(f32[8,2000]{1,0:T(8,128)} %shard_map.181) | data formatting | bytes 128000

commit v5 on v4

--- a/solution.py
+++ b/solution.py
@@ -291,20 +291,6 @@
 
     barrier = pltpu.get_barrier_semaphore()
 
-    def greet(k, carry):
-        other = lax.rem(me + k, n)
-        for side in (0, 1):
-            pl.semaphore_signal(
-                barrier,
-                inc=1,
-                device_id=(side, other // n_req, lax.rem(other, n_req)),
-                device_id_type=MESH,
-            )
-        return carry
-
-    lax.fori_loop(1, n, greet, 0)
-    pl.semaphore_signal(barrier, inc=1, device_id=(1 - cfg, blk, req), device_id_type=MESH)
-
     cache_copies = []
     for r in range(rows):
         for which, (source, target) in enumerate(((key_cache, keys), (value_cache, values))):
@@ -334,6 +320,20 @@
         weight_copies.append(
             pltpu.make_async_copy(source.at[pl.ds(0, extent)], target, sem)
         )
+
+    def greet(k, carry):
+        other = lax.rem(me + k, n)
+        for side in (0, 1):
+            pl.semaphore_signal(
+                barrier,
+                inc=1,
+                device_id=(side, other // n_req, lax.rem(other, n_req)),
+                device_id_type=MESH,
+            )
+        return carry
+
+    lax.fori_loop(1, n, greet, 0, unroll=True)
+    pl.semaphore_signal(barrier, inc=1, device_id=(1 - cfg, blk, req), device_id_type=MESH)
 
     upper = blk // 2
     near = (blk, 4 * upper + 1 - blk, 2 - upper, 3 - 3 * upper)
@@ -476,11 +476,6 @@
                 [block, stats], axis=0
             ).astype(BF16)
 
-    spot = (n - n_req, 2 * H, LANES)
-    empty = (lax.broadcasted_iota(jnp.int32, spot, 1) >= H) & (
-        lax.broadcasted_iota(jnp.int32, spot, 2) == 0
-    )
-    recv_a[1, pl.ds(n_req, n - n_req)] = jnp.where(empty, DEAD, 0.0).astype(BF16)
     pl.semaphore_wait(barrier, 2 * n - 1)
 
     @pl.when(cfg * blk == 0)
@@ -517,24 +512,24 @@
     def _():
         wait_plane(recv_a, n_req, sems_a.at[1])
 
-    for stream in (0, 1):
-        for q in range(n_req):
-            blocks = []
-            levels = []
-            for b in range(n_blk):
-                message = recv_a[stream, b * n_req + q].astype(F32)
-                levels.append(jnp.sum(message[H:], axis=1, keepdims=True))
-                blocks.append(message[:H])
-            peak = levels[0]
-            for b in range(1, n_blk):
-                peak = jnp.maximum(peak, levels[b])
-            total = jnp.zeros_like(peak)
-            mixed = jnp.zeros_like(blocks[0])
-            for b in range(n_blk):
-                weight = jnp.exp(levels[b] - peak)
-                total = total + weight
-                mixed = mixed + weight * blocks[b]
-            joint[pl.ds((stream * n_req + q) * H, H)] = mixed / total
+    for q in range(n_req):
+        blocks = []
+        levels = []
+        for b in range(n_blk):
+            message = recv_a[0, b * n_req + q].astype(F32)
+            levels.append(jnp.sum(message[H:], axis=1, keepdims=True))
+            blocks.append(message[:H])
+        peak = levels[0]
+        for b in range(1, n_blk):
+            peak = jnp.maximum(peak, levels[b])
+        total = jnp.zeros_like(peak)
+        mixed = jnp.zeros_like(blocks[0])
+        for b in range(n_blk):
+            weight = jnp.exp(levels[b] - peak)
+            total = total + weight
+            mixed = mixed + weight * blocks[b]
+        joint[pl.ds(q * H, H)] = mixed / total
+        joint[pl.ds((n_req + q) * H, H)] = recv_a[1, q, pl.ds(0, H)].astype(F32)
     gathered = jnp.concatenate(
         [joint[pl.ds(h, 2 * n_req * rows, stride=quarter), :] for h in range(quarter)], axis=1
     )

time: 49.5 us -> 49.6 us (level)
  no operation moved by 1% of the time
where the time goes in v5:
time: 49.6 us; the launch traced here: 49.4 us
  Pallas kernels  47.9 us (97%)
  local copies, waits for them, and re-layouts  1.47 us (3%)
    pallas_call x1, Pallas kernels, fused(): pl.pallas_call(lambda *refs: step_kernel(n_blk, n_req, *refs), out_shape=...  47.9 us
    unnamed x1, local copies, waits for them, and re-layouts  1.47 us

profile of v5, /device:TPU:0, one launch (start us, length us, event | category | flops | bytes accessed | tf_op | source)
XLA Modules:
  0.0 49.4 jit_solution(8150779894239186284)
XLA Ops:
  0.0 47.9 %shard_map.181 = f32[8,2000]{1,0:T(8,128)} custom-call(bf16[1,16,2048]{2,1,0:T(8,128)(2,1)} %refs_0_.1, bf16[1,4,4096]{2,1,0:T(4,128)(2,1)} %refs_1_.1, bf16[1,4,2,2048]{3,2,1,0:T(2,128)(2,1)} %refs_2_.1, bf16[1,4,48,2048]{3,2,1,0:T(8,128)(2,1)} %refs_3_.1, bf16[1,4,48,2048]{3,2,1,0:T(8,128)(2,1)} %refs_4_.1, s32[1,4]{1,0:T(1,128)} %refs_5_.1, ...), custom_call_target="tpu_custom_call" | custom-call | flops 751828992 | bytes 46989312 | tf_op jit(solution)/shard_map/pallas_call | solution.py:701
  47.9 1.5 %copy.21 = f32[8,2000]{1,0:T(8,128)} copy(f32[8,2000]{1,0:T(8,128)} %shard_map.181) | data formatting | bytes 128000
